TPU v7x, 256 devices: a whole 4x4x8 slice. The times are simulated.
256 devices in a mesh: rep: 32 (over z_hi, y, x), fsdp: 8 (over z_lo, core).
Axes of the slice: x: 4, y: 4, z: 8 (z_hi: 2, z_lo: 4; z = z_hi * 4 + z_lo), core: 2. Of those that a mesh axis runs over, the one named last changes fastest.
Arguments:
- hidden: bfloat16 [65536, 4608], P(('rep', 'fsdp')), may hold values from -12 to 12
- lengths: int32 [256, 8], P(('rep', 'fsdp')), may hold values from 1 to 64, 256 in all within a row
- ranks: int32 [256, 8], P(('rep', 'fsdp')), may hold values from 0 to 7, each once within a row
- gain: bfloat16 [4608], P('fsdp'), may hold values from 0.5 to 1.5
- head: bfloat16 [4608], P('fsdp'), may hold values from -1 to 1
- local_frag: bfloat16 [32, 512, 4608], P('rep', 'fsdp'), may hold values from -6 to 6
- global_prev: float32 [512, 4608], P('fsdp'), may hold values from -4 to 4
- momentum: float32 [512, 4608], P('fsdp'), may hold values from -3 to 3
Outputs:
- d_hidden: bfloat16 [65536, 4608], P(('rep', 'fsdp'))
- grad_gain: float32 [32, 4608], P('rep', 'fsdp')
- grad_head: float32 [32, 4608], P('rep', 'fsdp')
- new_global: float32 [512, 4608], P('fsdp')
- new_momentum: float32 [512, 4608], P('fsdp')
- merged: bfloat16 [32, 512, 4608], P('rep', 'fsdp')
Inputs may be any that keep to these rules, and one draw needn't show every extreme that they name: The 8 lengths of each list sum to 256, and the longest passage of each list has exactly 64 tokens. `ranks`: each row is a permutation of 0 to 7.
All inputs are finite; a program needn't handle non-finite values.
Results may differ from a plain program's by a relative error of at most 0.001.
Values may be sent and summed in bfloat16 or wider, within the bound.
No kernel may reach another device: no remote copies, remote signals or barrier semaphores. Data moves between devices by JAX's collectives and lax.ppermute only.
A program may use at most 64 MiB of HBM per device.

v0:
```python
import jax
import jax.numpy as jnp
from jax import lax
from jax.sharding import PartitionSpec as P

LIST_LEN = 256


SOFTCAP = 30.0
TEMPER = 2.0
LOSS_SCALE = 512.0
OUTER_RATE = 0.7
MOMENTUM = 0.9
MIXING = 0.5
EPSILON = 1e-06


def membership(lengths, list_len):
    ends = jnp.cumsum(lengths, axis=-1)
    starts = ends - lengths
    position = jnp.arange(list_len, dtype=jnp.int32)
    inside = (position[None, None, :] >= starts[:, :, None]) & (
        position[None, None, :] < ends[:, :, None]
    )
    return inside.astype(jnp.float32)


def head_work(hidden, lengths, ranks, gain, head):
    gain_full, head_full = (
        lax.all_gather(gain, "fsdp", axis=0, tiled=True),
        lax.all_gather(head, "fsdp", axis=0, tiled=True),
    )
    hidden_lists = hidden.reshape(hidden.shape[0] // LIST_LEN, LIST_LEN, hidden.shape[1])
    member = membership(lengths, LIST_LEN)
    values = hidden_lists.astype(jnp.float32)
    inverse = lax.rsqrt(jnp.mean(values * values, axis=-1, keepdims=True) + EPSILON)
    normal = values * inverse
    gain_wide = gain_full.astype(jnp.float32)
    head_wide = head_full.astype(jnp.float32)
    normed = normal * gain_wide
    root = jnp.sqrt(lengths.astype(jnp.float32))
    pooled = (
        jnp.einsum("lct,ltd->lcd", member, normed, precision=lax.Precision.HIGHEST)
        / root[:, :, None]
    )
    raw = jnp.einsum("lcd,d->lc", pooled, head_wide, precision=lax.Precision.HIGHEST)
    capped = SOFTCAP * jnp.tanh(raw / SOFTCAP)
    weights = jnp.exp(capped)
    probs = weights / jnp.sum(weights, axis=-1, keepdims=True)
    teacher = jnp.exp(-ranks.astype(jnp.float32) / TEMPER)
    target = teacher / jnp.sum(teacher, axis=-1, keepdims=True)
    slope = LOSS_SCALE * (probs - target) * (1.0 - (capped / SOFTCAP) ** 2)
    dpooled = slope[:, :, None] * head_wide[None, None, :] / root[:, :, None]
    dnormed = jnp.einsum("lct,lcd->ltd", member, dpooled, precision=lax.Precision.HIGHEST)
    gain_term = jnp.sum(dnormed * normal, axis=(0, 1)) / LOSS_SCALE
    head_term = jnp.einsum("lc,lcd->d", slope, pooled, precision=lax.Precision.HIGHEST) / LOSS_SCALE
    grad_gain, grad_head = (
        lax.psum_scatter(gain_term[None, :], "fsdp", scatter_dimension=1, tiled=True),
        lax.psum_scatter(head_term[None, :], "fsdp", scatter_dimension=1, tiled=True),
    )
    dnormal = dnormed * gain_wide
    dvalues = inverse * (dnormal - normal * jnp.mean(dnormal * normal, axis=-1, keepdims=True))
    d_hidden = dvalues.astype(jnp.bfloat16).reshape(hidden.shape)
    return (d_hidden, grad_gain, grad_head)


def outer_update(average, global_rows, momentum_rows):
    new_momentum = MOMENTUM * momentum_rows + average
    new_global = global_rows - OUTER_RATE * (MOMENTUM * new_momentum + average)
    return (new_global, new_momentum)


def outer_work(local_frag, global_prev, momentum):
    replicas = lax.axis_size("rep")
    local_wide = local_frag[0].astype(jnp.float32)
    outer = global_prev - local_wide
    total = lax.psum(outer, "rep")
    new_global, new_momentum = outer_update(total / replicas, global_prev, momentum)
    merged = (MIXING * local_wide + (1.0 - MIXING) * new_global).astype(jnp.bfloat16)[None, :, :]
    return (new_global, new_momentum, merged)


def body(hidden, lengths, ranks, gain, head, local_frag, global_prev, momentum):
    d_hidden, grad_gain, grad_head = head_work(hidden, lengths, ranks, gain, head)
    new_global, new_momentum, merged = outer_work(local_frag, global_prev, momentum)
    return (d_hidden, grad_gain, grad_head, new_global, new_momentum, merged)


def solution(mesh):
    placed = (
        P(("rep", "fsdp"), None),
        P(("rep", "fsdp"), None),
        P(("rep", "fsdp"), None),
        P("fsdp"),
        P("fsdp"),
        P("rep", "fsdp", None),
        P("fsdp", None),
        P("fsdp", None),
    )
    return jax.shard_map(
        body,
        mesh=mesh,
        in_specs=placed,
        out_specs=(
            P(("rep", "fsdp"), None),
            P("rep", "fsdp"),
            P("rep", "fsdp"),
            P("fsdp", None),
            P("fsdp", None),
            P("rep", "fsdp", None),
        ),
        check_vma=False,
    )
```

profile of v0, /device:TPU:32, one launch (start us, length us, event | category | flops | bytes accessed | tf_op | source)
XLA Modules:
  0.0 505.7 jit_solution(17872122064396250616)
XLA Ops:
  8.0 0.0 copy-start
  8.0 0.0 copy-start.4
  8.0 0.0 copy-start.3
  8.0 0.0 reduce-scatter.7.cloned.1.call-start
  8.1 1.4 dynamic-slice
  10.2 0.9 dynamic-update-slice
  11.0 0.9 dynamic-update-slice.1
  11.9 25.9 %all-reduce.2 = (bf16[4608]{0:T(1024)(128)(2,1)S(1)}, bf16[4608]{0:T(1024)(128)(2,1)S(1)}) all-reduce(bf16[4608]{0:T(1024)(128)(2,1)S(1)} %dynamic-update-slice.1, bf16[4608]{0:T(1024)(128)(2,1)S(1)} %dynamic-update-slice), channel_id=1, replica_groups=mesh['rep'=32,'fsdp'=8] {'fsdp'}, use_global_device_ids=true, to_apply=%add.1 | all-reduce | flops 9216 | bytes 36864
  37.8 0.0 copy-start.2
  37.8 2.2 fusion.10
  40.1 0.0 copy-done.4
  40.1 0.2 reduce_window_sum.11
  40.3 0.0 copy-done.3
  40.3 0.6 fusion.33
  40.9 0.0 copy-done
  40.9 2.1 convolution_divide_fusion
  43.0 0.9 fusion.32
  43.9 1.3 bitcast_multiply_fusion
  45.2 0.0 copy-done.2
  45.2 5.1 %fusion.9 = (f32[4608]{0:T(1024)S(1)}, f32[256]{0:T(256)S(1)}, f32[256,4608]{1,0:T(8,128)}) fusion(bf16[256,4608]{1,0:T(8,128)(2,1)S(1)} %copy-done, f32[256]{0:T(256)S(1)} %add_rsqrt_fusion, f32[4608]{0:T(1024)S(1)} %convert_element_type.31, f32[4608]{0:T(1024)S(1)} %convert_element_type.34, f32[8]{0:T(128)S(1)} %bitcast.39, f32[8]{0:T(128)S(1)} %sqrt_bitcast_fusion, ...), kind=kOutput, calls=%fused_computation.11 | convolution fusion | flops 121578752 | bytes 7135360 | tf_op jit(solution)/shard_map/lct,lcd->ltd/dot_general | solution.py:54
  50.3 3.0 reshape_bitcast_fusion.1
  53.3 0.0 reduce-scatter.7.cloned.1.call-update
  53.3 0.0 reduce-scatter.9.cloned.1.call-start
  53.3 0.3 convolution_reduce_fusion
  53.7 0.0 copy-start.1
  53.7 3.1 reshape_bitcast_fusion
  56.8 0.0 reduce-scatter.9.cloned.1.call-update
  56.8 0.0 all-reduce.5.cloned.1.call-start
  56.8 0.0 copy-done.1
  56.8 2.2 convert_subtract_fusion
  59.0 0.0 all-reduce.5.cloned.1.call-update
  59.1 5.0 fusion.8
  64.1 32.4 %reduce-scatter.7.cloned.1.call-done = f32[576,1]{1,0:T(8,128)} async-done(((f32[4608,1]{1,0:T(8,128)}), f32[576,1]{1,0:T(8,128)}) %reduce-scatter.7.cloned.1.call-update) | async-done | bytes 2320
  96.4 1.7 copy.15
  98.1 43.0 %reduce-scatter.9.cloned.1.call-done = f32[576,1]{1,0:T(8,128)} async-done(((f32[4608,1]{1,0:T(8,128)}), f32[576,1]{1,0:T(8,128)}) %reduce-scatter.9.cloned.1.call-update) | async-done | bytes 2320
  141.2 1.7 copy.17
  142.9 351.7 %all-reduce.5.cloned.1.call-done = f32[64,4608]{1,0:T(8,128)} async-done(((f32[64,4608]{1,0:T(8,128)}), f32[64,4608]{1,0:T(8,128)}) %all-reduce.5.cloned.1.call-update) | async-done | bytes 1179664 | tf_op jit(solution)/shard_map/psum | solution.py:77
  494.6 3.7 fusion.17
  (11 shorter events, 0.1 us)
Async XLA Ops:
  8.0 32.9 %copy-start = (bf16[256,4608]{1,0:T(8,128)(2,1)S(1)}, bf16[256,4608]{1,0:T(8,128)(2,1)}, u32[]{:S(2)}) copy-start(bf16[256,4608]{1,0:T(8,128)(2,1)} %param.8) | copy-start | bytes 7077892
  8.0 32.0 %copy-start.4 = (s32[1,8]{1,0:T(1,128)S(1)}, s32[1,8]{1,0:T(1,128)}, u32[]{:S(2)}) copy-start(s32[1,8]{1,0:T(1,128)} %param.9) | copy-start | bytes 100
  8.0 32.3 %copy-start.3 = (s32[1,8]{1,0:T(1,128)S(1)}, s32[1,8]{1,0:T(1,128)}, u32[]{:S(2)}) copy-start(s32[1,8]{1,0:T(1,128)} %param.10) | copy-start | bytes 100
  8.0 88.4 %reduce-scatter.7.cloned.1.call-start = ((), (), s32[]{:S(2)}) async-start(), calls=%async_computation.3 | async-start | bytes 2654208
  37.8 7.3 %copy-start.2 = (f32[4608]{0:T(1024)}, f32[4608]{0:T(1024)S(1)}, u32[]{:S(2)}) copy-start(f32[4608]{0:T(1024)S(1)} %convert_element_type.31) | copy-start | bytes 55300
  53.3 87.9 %reduce-scatter.9.cloned.1.call-start = ((), (), s32[]{:S(2)}) async-start(), calls=%async_computation.4 | async-start | bytes 2654208
  53.7 3.2 copy-start.1
  56.8 437.8 %all-reduce.5.cloned.1.call-start = ((), (), s32[]{:S(2)}) async-start(), calls=%async_computation.2 | async-start | bytes 2359296 | tf_op jit(solution)/shard_map/psum | solution.py:77
Sparse Core Ops, SparseCore 0:
  53.4 42.9 reduce-scatter.6
  99.0 42.1 reduce-scatter.8
Sparse Core Ops, SparseCore 1:
  60.5 434.0 all-reduce.4
where the time goes:
time: 506 us
  waiting for transfers between devices  427 us (84%)
  blocking collectives  25.9 us (5%)
  between operations  16.3 us (3%)
  other arithmetic  15.3 us (3%)
  local copies, waits for them, and re-layouts  12.6 us (2%)
  matrix products  8.4 us (2%)
    psum x1, waiting for transfers between devices, outer_work(): total = lax.psum(outer, 'rep')  352 us
    unnamed x5, waiting for transfers between devices  75.5 us
    unnamed x1, blocking collectives  25.9 us
    unnamed x20, local copies, waits for them, and re-layouts  12.6 us
  transfers between devices with their start and end apart: 3, of which 3 were waited for; matrix products, arithmetic and copies ran while one was open for 3% of the time, Pallas kernels for 0%

commit v1 on v0

v1 whole, which is shorter than its diff:
```python
import jax
import jax.numpy as jnp
from jax import lax
from jax.experimental import pallas as pl
from jax.experimental.pallas import tpu as pltpu
from jax.sharding import PartitionSpec as P

LIST_LEN = 256
CAND = 8
LANES = 128
ROWS = 32

SOFTCAP = 30.0
TEMPER = 2.0
LOSS_SCALE = 512.0
OUTER_RATE = 0.7
MOMENTUM = 0.9
MIXING = 0.5
EPSILON = 1e-06

PLANES = 2
PLANE = 16


def head_kernel(lengths_ref, ranks_ref, hidden_ref, v_ref, out_ref, w_ref, square_ref, dot_ref):
    tokens, width = hidden_ref.shape

    def first(step, carry):
        rows = pl.ds(pl.multiple_of(step * ROWS, ROWS), ROWS)
        values = hidden_ref[rows, :].astype(jnp.float32)
        square_ref[rows, :] = jnp.sum(values * values, axis=1, keepdims=True)
        dot_ref[rows, :] = jnp.sum(values * v_ref[...], axis=1, keepdims=True)
        return carry

    lax.fori_loop(0, tokens // ROWS, first, 0)

    inverse = lax.rsqrt(square_ref[...] / width + EPSILON)
    dots = dot_ref[...]

    lane = lax.broadcasted_iota(jnp.int32, (1, LANES), 1)
    starts = jnp.zeros((1, LANES), jnp.int32)
    ends = jnp.zeros((1, LANES), jnp.int32)
    ranks = jnp.zeros((1, LANES), jnp.int32)
    end = jnp.int32(0)
    for c in range(CAND):
        start, end = end, end + lengths_ref[0, c]
        starts = jnp.where(lane == c, start, starts)
        ends = jnp.where(lane == c, end, ends)
        ranks = jnp.where(lane == c, ranks_ref[0, c], ranks)
    real = lane < CAND
    root = jnp.sqrt(jnp.where(real, ends - starts, 1).astype(jnp.float32))
    position = lax.broadcasted_iota(jnp.int32, (tokens, LANES), 0)
    member = (position >= starts) & (position < ends)

    raw = jnp.sum(jnp.where(member, inverse * dots, 0.0), axis=0, keepdims=True) / root
    capped = SOFTCAP * jnp.tanh(raw / SOFTCAP)
    weights = jnp.where(real, jnp.exp(capped), 0.0)
    probs = weights / jnp.sum(weights, axis=1, keepdims=True)
    teacher = jnp.where(real, jnp.exp(-ranks.astype(jnp.float32) / TEMPER), 0.0)
    target = teacher / jnp.sum(teacher, axis=1, keepdims=True)
    slope = LOSS_SCALE * (probs - target) * (1.0 - (capped / SOFTCAP) ** 2)
    scale = jnp.sum(jnp.where(member, slope / root, 0.0), axis=1, keepdims=True)

    alpha = inverse * scale
    square_ref[...] = alpha
    dot_ref[...] = alpha * inverse * inverse * dots / width
    w_ref[...] = jnp.zeros_like(w_ref)

    def second(step, carry):
        rows = pl.ds(pl.multiple_of(step * ROWS, ROWS), ROWS)
        values = hidden_ref[rows, :].astype(jnp.float32)
        alphas = square_ref[rows, :]
        out_ref[rows, :] = (alphas * v_ref[...] - dot_ref[rows, :] * values).astype(out_ref.dtype)
        w_ref[...] += jnp.sum(alphas * values, axis=0, keepdims=True)
        return carry

    lax.fori_loop(0, tokens // ROWS, second, 0)
    w_ref[...] = w_ref[...] / LOSS_SCALE


def head_call(hidden, lengths, ranks, v):
    tokens, width = hidden.shape
    smem = pl.BlockSpec(memory_space=pltpu.SMEM)
    vmem = pl.BlockSpec(memory_space=pltpu.VMEM)
    return pl.pallas_call(
        head_kernel,
        out_shape=(
            jax.ShapeDtypeStruct((tokens, width), jnp.bfloat16),
            jax.ShapeDtypeStruct((1, width), jnp.float32),
        ),
        in_specs=[smem, smem, vmem, vmem],
        out_specs=(vmem, vmem),
        scratch_shapes=[pltpu.VMEM((tokens, 1), jnp.float32), pltpu.VMEM((tokens, 1), jnp.float32)],
        compiler_params=pltpu.CompilerParams(vmem_limit_bytes=24 * 1024 * 1024),
        cost_estimate=pl.CostEstimate(flops=10 * tokens * width, bytes_accessed=4 * tokens * width, transcendentals=0),
        name="head",
    )(lengths, ranks, hidden, v)


def head_work(hidden, lengths, ranks, gain, head):
    devices = lax.axis_size("fsdp")
    gain_wide, head_wide = gain.astype(jnp.float32), head.astype(jnp.float32)
    own = gain_wide * head_wide
    v = lax.all_to_all(
        jnp.broadcast_to(own[None, :], (devices, own.shape[0])), "fsdp", 0, 0, tiled=True
    ).reshape(1, hidden.shape[1])
    d_hidden, w = head_call(hidden, lengths, ranks, v)
    w = lax.all_to_all(w.reshape(devices, own.shape[0]), "fsdp", 0, 0, tiled=True)
    w = jnp.sum(w, axis=0)
    return d_hidden, (w * head_wide)[None, :], (w * gain_wide)[None, :]


def outer_work(local_frag, global_prev, momentum):
    rows, width = global_prev.shape
    replicas = lax.axis_size("rep")
    planes = [[PLANE * z + i for i in range(PLANE)] for z in range(PLANES)]
    other_plane = [(i, (i + PLANE) % replicas) for i in range(replicas)]
    piece = rows // PLANE
    local = local_frag[0]
    mine = lax.all_to_all(
        local.reshape(PLANE, piece, width), "rep", 0, 0, tiled=True, axis_index_groups=planes
    )
    partial = jnp.sum(mine.astype(jnp.float32), axis=0)
    total = partial + lax.ppermute(partial, "rep", other_plane)
    at = lax.rem(lax.axis_index("rep"), PLANE) * piece
    average = lax.dynamic_slice_in_dim(global_prev, at, piece, 0) - total / replicas
    average = lax.all_to_all(
        jnp.broadcast_to(average[None], (PLANE, piece, width)), "rep", 0, 0, tiled=True, axis_index_groups=planes
    ).reshape(rows, width)
    new_momentum = MOMENTUM * momentum + average
    new_global = global_prev - OUTER_RATE * (MOMENTUM * new_momentum + average)
    merged = (MIXING * local.astype(jnp.float32) + (1.0 - MIXING) * new_global).astype(jnp.bfloat16)
    return new_global, new_momentum, merged[None]


def body(hidden, lengths, ranks, gain, head, local_frag, global_prev, momentum):
    d_hidden, grad_gain, grad_head = head_work(hidden, lengths, ranks, gain, head)
    new_global, new_momentum, merged = outer_work(local_frag, global_prev, momentum)
    return d_hidden, grad_gain, grad_head, new_global, new_momentum, merged


def solution(mesh):
    placed = (
        P(("rep", "fsdp"), None),
        P(("rep", "fsdp"), None),
        P(("rep", "fsdp"), None),
        P("fsdp"),
        P("fsdp"),
        P("rep", "fsdp", None),
        P("fsdp", None),
        P("fsdp", None),
    )
    return jax.shard_map(
        body,
        mesh=mesh,
        in_specs=placed,
        out_specs=(
            P(("rep", "fsdp"), None),
            P("rep", "fsdp"),
            P("rep", "fsdp"),
            P("fsdp", None),
            P("fsdp", None),
            P("rep", "fsdp", None),
        ),
        check_vma=False,
    )
```

time: 506 us -> 82 us (0.16)
  the two profiles are of different devices: /device:TPU:32 before, /device:TPU:1 now
where the time goes in v1:
time: 82 us; the launch traced here: 81.6 us
  waiting for transfers between devices  25.4 us (31%)
  starting transfers between devices  20.1 us (25%)
  blocking collectives  18.8 us (23%)
  Pallas kernels  6.15 us (8%)
  local copies, waits for them, and re-layouts  5.51 us (7%)
  other arithmetic  4.88 us (6%)
    all_to_all x1, blocking collectives, outer_work(): lax.all_to_all(local.reshape(PLANE, piece, width), 'rep', 0, 0, tiled=Tru...  18.8 us
    all_to_all x1, waiting for transfers between devices, outer_work(): lax.all_to_all(jnp.broadcast_to(average[None], (PLANE, piece, width)), 'r...  16.4 us
    ppermute x1, starting transfers between devices, outer_work(): total = partial + lax.ppermute(partial, 'rep', other_plane)  6.99 us
    pallas_call x1, Pallas kernels, head_call(): pl.pallas_call(head_kernel, out_shape=(jax.ShapeDtypeStruct((tokens, widt...  6.15 us
    all_to_all x1, starting transfers between devices, head_work(): lax.all_to_all(jnp.broadcast_to(own[None, :], (devices, own.shape[0])), '...  5.47 us
    all_to_all x1, waiting for transfers between devices, head_work(): lax.all_to_all(jnp.broadcast_to(own[None, :], (devices, own.shape[0])), '...  4.97 us
    all_to_all x1, waiting for transfers between devices, head_work(): lax.all_to_all(w.reshape(devices, own.shape[0]), 'fsdp', 0, 0, tiled=True)  4.02 us
    all_to_all x1, starting transfers between devices, head_work(): lax.all_to_all(w.reshape(devices, own.shape[0]), 'fsdp', 0, 0, tiled=True)  3.98 us
  transfers between devices with their start and end apart: 4, of which 3 were waited for; matrix products, arithmetic and copies ran while one was open for 4% of the time, Pallas kernels for 8%

profile of v1, /device:TPU:1, one launch (start us, length us, event | category | flops | bytes accessed | tf_op | source)
XLA Modules:
  0.0 81.6 jit_solution(4669203169264558375)
XLA Ops:
  0.6 0.0 copy-start
  0.6 1.4 %reshape_squeeze.3 = bf16[16,4,4608]{2,1,0:T(4,128)(2,1)S(1)} reshape(bf16[1,64,4608]{2,1,0:T(8,128)(2,1)} %param.13) | data formatting | bytes 1179648 | tf_op jit(solution)/shard_map/reshape;squeeze | solution.py:121
  2.0 0.0 copy-start.4
  2.0 0.0 copy-start.5
  2.0 0.0 copy-start.1
  2.0 0.0 copy-start.2
  2.0 18.8 %all_to_all.26 = bf16[16,4,4608]{2,1,0:T(4,128)(2,1)S(1)} all-to-all(bf16[16,4,4608]{2,1,0:T(4,128)(2,1)S(1)} %reshape_squeeze.3), channel_id=1, replica_groups={{0,8,16,24,32,40,48,56,64,72,80,88,96,104,112,120},{128,136,144,152,160..., dimensions={0} | all-to-all | bytes 1179648 | tf_op jit(solution)/shard_map/all_to_all | solution.py:120
  20.8 0.2 convert_reduce_fusion
  21.1 7.0 %collective-permute-start = (f32[4,4608]{1,0:T(4,128)S(1)}, f32[4,4608]{1,0:T(4,128)S(1)}, u32[]{:S(2)}, u32[]{:S(2)}) collective-permute-start(f32[4,4608]{1,0:T(4,128)S(1)} %convert_reduce_fusion), channel_id=1, source_target_pairs={{0,128},{8,136},{16,144},{24,152},{32,160},{40,168},{48,176},{56,1... | collective-permute-start | bytes 221192 | tf_op jit(solution)/shard_map/ppermute | solution.py:124
  28.1 0.0 copy-done.4
  28.1 0.0 copy-done.5
  28.1 0.6 broadcast_in_dim.10
  28.7 5.5 %all-to-all-start = ((f32[8,1,576]{2,1,0:T(1,128)}), f32[8,1,576]{2,1,0:T(1,128)S(1)}, u32[]{:S(2)}, u32[]{:S(2)}) async-start(f32[8,1,576]{2,1,0:T(1,128)} %broadcast_in_dim.10), calls=%async_computation | async-start | bytes 40960 | tf_op jit(solution)/shard_map/all_to_all | solution.py:104
  34.2 5.0 %all-to-all-done = f32[8,1,576]{2,1,0:T(1,128)S(1)} async-done(((f32[8,1,576]{2,1,0:T(1,128)}), f32[8,1,576]{2,1,0:T(1,128)S(1)}, u32[]{:S(2)}, u32[]{:S(2)}) %all-to-all-start) | async-done | bytes 18464 | tf_op jit(solution)/shard_map/all_to_all | solution.py:104
  39.2 0.1 reshape.32.v_ref
  39.3 0.0 copy-done
  39.3 0.0 copy-done.1
  39.3 0.0 copy-done.2
  39.3 6.1 %head.1 = (bf16[256,4608]{1,0:T(8,128)(2,1)}, f32[1,4608]{1,0:T(1,128)S(1)}) custom-call(s32[1,8]{1,0:T(1,128)S(1)} %copy-done.1, s32[1,8]{1,0:T(1,128)S(1)} %copy-done.2, bf16[256,4608]{1,0:T(8,128)(2,1)S(1)} %copy-done, f32[1,4608]{1,0:T(1,128)S(1)} %reshape.32.v_ref), custom_call_target="tpu_custom_call" | custom-call | flops 11796480 | bytes 4718592 | tf_op jit(solution)/shard_map/head/pallas_call | solution.py:85
  45.5 0.7 all_to_all.21
  46.2 4.0 %all-to-all-start.1 = ((f32[8,1,576]{2,1,0:T(1,128)}), f32[8,1,576]{2,1,0:T(1,128)S(1)}, u32[]{:S(2)}, u32[]{:S(2)}) async-start(f32[8,1,576]{2,1,0:T(1,128)} %all_to_all.21), calls=%async_computation.1 | async-start | bytes 40960 | tf_op jit(solution)/shard_map/all_to_all | solution.py:108
  50.2 0.0 collective-permute-done
  50.2 0.9 %multiply_subtract_fusion.1 = f32[4,4608]{1,0:T(4,128)S(1)} fusion(f32[4,4608]{1,0:T(4,128)S(1)} %convert_reduce_fusion, f32[4,4608]{1,0:T(4,128)S(1)} %collective-permute-done, f32[64,4608]{1,0:T(8,128)} %param.14, s32[]{:T(128)S(6)} %select_n.3), kind=kLoop, calls=%fused_computation.7 | loop fusion | flops 55296 | bytes 294916 | tf_op jit(solution)/shard_map/sub | solution.py:126
  51.1 4.0 %all-to-all-done.1 = f32[8,1,576]{2,1,0:T(1,128)S(1)} async-done(((f32[8,1,576]{2,1,0:T(1,128)}), f32[8,1,576]{2,1,0:T(1,128)S(1)}, u32[]{:S(2)}, u32[]{:S(2)}) %all-to-all-start.1) | async-done | bytes 18464 | tf_op jit(solution)/shard_map/all_to_all | solution.py:108
  55.1 1.2 %broadcast_in_dim.24 = f32[16,4,4608]{2,1,0:T(4,128)} broadcast(f32[4,4608]{1,0:T(4,128)S(1)} %multiply_subtract_fusion.1), dimensions={1,2} | broadcast | bytes 1253376 | tf_op jit(solution)/shard_map/broadcast_in_dim | solution.py:128
  56.3 3.7 %all-to-all-start.3 = ((f32[16,4,4608]{2,1,0:T(4,128)}), f32[16,4,4608]{2,1,0:T(4,128)S(1)}, u32[]{:S(2)}, u32[]{:S(2)}) async-start(f32[16,4,4608]{2,1,0:T(4,128)} %broadcast_in_dim.24), calls=%async_computation.3 | async-start | bytes 2359296 | tf_op jit(solution)/shard_map/all_to_all | solution.py:127
  60.1 0.6 broadcast_in_dim.22
  60.6 0.6 broadcast_in_dim.23
  61.2 0.0 copy-start.3
  61.2 16.4 %all-to-all-done.3 = f32[16,4,4608]{2,1,0:T(4,128)S(1)} async-done(((f32[16,4,4608]{2,1,0:T(4,128)}), f32[16,4,4608]{2,1,0:T(4,128)S(1)}, u32[]{:S(2)}, u32[]{:S(2)}) %all-to-all-start.3) | async-done | bytes 1179680 | tf_op jit(solution)/shard_map/all_to_all | solution.py:127
  77.6 0.4 reshape.33
  78.0 0.0 copy-done.3
  78.1 3.6 %fusion.2 = (bf16[1,64,4608]{2,1,0:T(8,128)(2,1)}, f32[64,4608]{1,0:T(8,128)}, f32[64,4608]{1,0:T(8,128)}) fusion(bf16[1,64,4608]{2,1,0:T(8,128)(2,1)S(1)} %copy-done.3, f32[64,4608]{1,0:T(8,128)} %param.14, f32[64,4608]{1,0:T(8,128)S(1)} %reshape.33, f32[64,4608]{1,0:T(8,128)} %param.15), kind=kLoop, calls=%fused_computation.6 | loop fusion | flops 2949120 | bytes 7077888 | tf_op jit(solution)/shard_map/broadcast_in_dim | solution.py:133
  (5 shorter events, 0.1 us)
Async XLA Ops:
  0.6 38.6 %copy-start = (bf16[256,4608]{1,0:T(8,128)(2,1)S(1)}, bf16[256,4608]{1,0:T(8,128)(2,1)}, u32[]{:S(2)}) copy-start(bf16[256,4608]{1,0:T(8,128)(2,1)} %hidden_ref.1) | copy-start | bytes 7077892
  2.0 26.1 %copy-start.4 = (bf16[576]{0:T(1024)(128)(2,1)S(1)}, bf16[576]{0:T(1024)(128)(2,1)}, u32[]{:S(2)}) copy-start(bf16[576]{0:T(1024)(128)(2,1)} %param.12) | copy-start | bytes 3460
  2.0 26.1 %copy-start.5 = (bf16[576]{0:T(1024)(128)(2,1)S(1)}, bf16[576]{0:T(1024)(128)(2,1)}, u32[]{:S(2)}) copy-start(bf16[576]{0:T(1024)(128)(2,1)} %param.11) | copy-start | bytes 3460
  2.0 37.3 %copy-start.1 = (s32[1,8]{1,0:T(1,128)S(1)}, s32[1,8]{1,0:T(1,128)}, u32[]{:S(2)}) copy-start(s32[1,8]{1,0:T(1,128)} %lengths_ref.1) | copy-start | bytes 100
  2.0 37.3 %copy-start.2 = (s32[1,8]{1,0:T(1,128)S(1)}, s32[1,8]{1,0:T(1,128)}, u32[]{:S(2)}) copy-start(s32[1,8]{1,0:T(1,128)} %ranks_ref.1) | copy-start | bytes 100
  21.1 29.1 %collective-permute-start = (f32[4,4608]{1,0:T(4,128)S(1)}, f32[4,4608]{1,0:T(4,128)S(1)}, u32[]{:S(2)}, u32[]{:S(2)}) collective-permute-start(f32[4,4608]{1,0:T(4,128)S(1)} %convert_reduce_fusion), channel_id=1, source_target_pairs={{0,128},{8,136},{16,144},{24,152},{32,160},{40,168},{48,176},{56,1... | collective-permute-start | bytes 221192 | tf_op jit(solution)/shard_map/ppermute | solution.py:124
  28.7 10.4 %all-to-all-start = ((f32[8,1,576]{2,1,0:T(1,128)}), f32[8,1,576]{2,1,0:T(1,128)S(1)}, u32[]{:S(2)}, u32[]{:S(2)}) async-start(f32[8,1,576]{2,1,0:T(1,128)} %broadcast_in_dim.10), calls=%async_computation | async-start | bytes 40960 | tf_op jit(solution)/shard_map/all_to_all | solution.py:104
  46.2 9.0 %all-to-all-start.1 = ((f32[8,1,576]{2,1,0:T(1,128)}), f32[8,1,576]{2,1,0:T(1,128)S(1)}, u32[]{:S(2)}, u32[]{:S(2)}) async-start(f32[8,1,576]{2,1,0:T(1,128)} %all_to_all.21), calls=%async_computation.1 | async-start | bytes 40960 | tf_op jit(solution)/shard_map/all_to_all | solution.py:108
  56.3 21.3 %all-to-all-start.3 = ((f32[16,4,4608]{2,1,0:T(4,128)}), f32[16,4,4608]{2,1,0:T(4,128)S(1)}, u32[]{:S(2)}, u32[]{:S(2)}) async-start(f32[16,4,4608]{2,1,0:T(4,128)} %broadcast_in_dim.24), calls=%async_computation.3 | async-start | bytes 2359296 | tf_op jit(solution)/shard_map/all_to_all | solution.py:127
  61.2 16.8 %copy-start.3 = (bf16[1,64,4608]{2,1,0:T(8,128)(2,1)S(1)}, bf16[1,64,4608]{2,1,0:T(8,128)(2,1)}, u32[]{:S(2)}) copy-start(bf16[1,64,4608]{2,1,0:T(8,128)(2,1)} %param.13) | copy-start | bytes 1769476

commit v2 on v1

v2 whole, which is shorter than its diff:
```python
import jax
import jax.numpy as jnp
from jax import lax
from jax.experimental import pallas as pl
from jax.experimental.pallas import tpu as pltpu
from jax.sharding import PartitionSpec as P

LIST_LEN = 256
CAND = 8
LANES = 128
ROWS = 32

SOFTCAP = 30.0
TEMPER = 2.0
LOSS_SCALE = 512.0
OUTER_RATE = 0.7
MOMENTUM = 0.9
MIXING = 0.5
EPSILON = 1e-06

PLANES = 2
PLANE = 16


def score_kernel(place_ref, lengths_ref, ranks_ref, hidden_ref, own_ref, one_ref, two_ref, three_ref,
                 w_ref, alpha_ref, beta_ref, v_ref, scale_ref):
    tokens, width = hidden_ref.shape
    block = own_ref.shape[1]
    place = place_ref[0, 0]
    columns = [pl.ds(pl.multiple_of((place ^ k) * block, LANES), block) for k in range(4)]
    for part, ref in zip(columns, (own_ref, one_ref, two_ref, three_ref)):
        v_ref[:, part] = ref[...]

    def first(step, carry):
        rows = pl.ds(pl.multiple_of(step * ROWS, ROWS), ROWS)
        square = jnp.zeros((ROWS, LANES), jnp.float32)
        dot = jnp.zeros((ROWS, LANES), jnp.float32)
        for j in range(width // LANES):
            part = slice(j * LANES, (j + 1) * LANES)
            values = hidden_ref[rows, part].astype(jnp.float32)
            square += values * values
            dot += values * v_ref[:, part]
        alpha_ref[rows, :] = jnp.sum(square, axis=1, keepdims=True)
        beta_ref[rows, :] = jnp.sum(dot, axis=1, keepdims=True)
        return carry

    lax.fori_loop(0, tokens // ROWS, first, 0)

    inverse = lax.rsqrt(alpha_ref[...] / width + EPSILON)
    dots = beta_ref[...]

    lane = lax.broadcasted_iota(jnp.int32, (1, LANES), 1)
    starts = jnp.zeros((1, LANES), jnp.int32)
    ends = jnp.zeros((1, LANES), jnp.int32)
    ranks = jnp.zeros((1, LANES), jnp.int32)
    end = jnp.int32(0)
    for c in range(CAND):
        start, end = end, end + lengths_ref[0, c]
        starts = jnp.where(lane == c, start, starts)
        ends = jnp.where(lane == c, end, ends)
        ranks = jnp.where(lane == c, ranks_ref[0, c], ranks)
    real = lane < CAND
    root = jnp.sqrt(jnp.where(real, ends - starts, 1).astype(jnp.float32))
    position = lax.broadcasted_iota(jnp.int32, (tokens, LANES), 0)
    member = (position >= starts) & (position < ends)

    raw = jnp.sum(jnp.where(member, inverse * dots, 0.0), axis=0, keepdims=True) / root
    capped = SOFTCAP * jnp.tanh(raw / SOFTCAP)
    weights = jnp.where(real, jnp.exp(capped), 0.0)
    probs = weights / jnp.sum(weights, axis=1, keepdims=True)
    teacher = jnp.where(real, jnp.exp(-ranks.astype(jnp.float32) / TEMPER), 0.0)
    target = teacher / jnp.sum(teacher, axis=1, keepdims=True)
    slope = LOSS_SCALE * (probs - target) * (1.0 - (capped / SOFTCAP) ** 2)
    scale = jnp.sum(jnp.where(member, slope / root, 0.0), axis=1, keepdims=True)

    alpha = inverse * scale
    alpha_ref[...] = alpha
    beta_ref[...] = alpha * inverse * inverse * dots / width
    scale_ref[...] = jnp.broadcast_to(alpha, scale_ref.shape)

    for k, columns_k in enumerate(columns):
        for j in range(block // LANES):
            at = pl.multiple_of((place ^ k) * block + j * LANES, LANES)
            total = jnp.zeros((ROWS, LANES), jnp.float32)
            for row in range(0, tokens, ROWS):
                values = hidden_ref[row:row + ROWS, pl.ds(at, LANES)].astype(jnp.float32)
                total += values * scale_ref[row:row + ROWS, :]
            w_ref[k:k + 1, j * LANES:(j + 1) * LANES] = jnp.sum(total, axis=0, keepdims=True) / LOSS_SCALE


def score_call(place, lengths, ranks, hidden, blocks):
    tokens, width = hidden.shape
    block = width // 4
    smem = pl.BlockSpec(memory_space=pltpu.SMEM)
    vmem = pl.BlockSpec(memory_space=pltpu.VMEM)
    column = jax.ShapeDtypeStruct((tokens, 1), jnp.float32)
    return pl.pallas_call(
        score_kernel,
        out_shape=(jax.ShapeDtypeStruct((4, block), jnp.float32), column, column,
                   jax.ShapeDtypeStruct((1, width), jnp.float32)),
        in_specs=[smem, smem, smem, vmem, vmem, vmem, vmem, vmem],
        out_specs=(vmem, vmem, vmem, vmem),
        scratch_shapes=[pltpu.VMEM((tokens, LANES), jnp.float32)],
        compiler_params=pltpu.CompilerParams(vmem_limit_bytes=16 * 1024 * 1024),
        cost_estimate=pl.CostEstimate(flops=6 * tokens * width, bytes_accessed=2 * tokens * width, transcendentals=0),
        name="score",
    )(place, lengths, ranks, hidden, *blocks)


def token_kernel(hidden_ref, v_ref, alpha_ref, beta_ref, out_ref):
    for j in range(hidden_ref.shape[1] // LANES):
        part = slice(j * LANES, (j + 1) * LANES)
        values = hidden_ref[:, part].astype(jnp.float32)
        out_ref[:, part] = (alpha_ref[...] * v_ref[:, part] - beta_ref[...] * values).astype(out_ref.dtype)


def token_call(hidden, v, alpha, beta):
    tokens, width = hidden.shape
    step = 64
    return pl.pallas_call(
        token_kernel,
        grid=(tokens // step,),
        out_shape=jax.ShapeDtypeStruct((tokens, width), jnp.bfloat16),
        in_specs=[
            pl.BlockSpec((step, width), lambda i: (i, 0)),
            pl.BlockSpec((1, width), lambda i: (0, 0)),
            pl.BlockSpec((step, 1), lambda i: (i, 0)),
            pl.BlockSpec((step, 1), lambda i: (i, 0)),
        ],
        out_specs=pl.BlockSpec((step, width), lambda i: (i, 0)),
        compiler_params=pltpu.CompilerParams(vmem_limit_bytes=16 * 1024 * 1024),
        cost_estimate=pl.CostEstimate(flops=4 * tokens * width, bytes_accessed=4 * tokens * width, transcendentals=0),
        name="token_grad",
    )(hidden, v, alpha, beta)


def along(array, k):
    devices = lax.axis_size("fsdp")
    return lax.ppermute(array, "fsdp", [(i, i ^ k) for i in range(devices)])


def outer_reduce(local):
    rows, width = local.shape
    planes = [[PLANE * z + i for i in range(PLANE)] for z in range(PLANES)]
    return lax.all_to_all(
        local.reshape(PLANE, rows // PLANE, width), "rep", 0, 0, tiled=True, axis_index_groups=planes
    )


def outer_average(total, global_prev):
    piece = total.shape[0]
    at = lax.rem(lax.axis_index("rep"), PLANE) * piece
    return lax.dynamic_slice_in_dim(global_prev, at, piece, 0) - total / lax.axis_size("rep")


def outer_spread(average):
    planes = [[PLANE * z + i for i in range(PLANE)] for z in range(PLANES)]
    sent = jnp.broadcast_to(average.astype(jnp.float16)[None], (PLANE, *average.shape))
    return sent, lambda sent: lax.all_to_all(sent, "rep", 0, 0, tiled=True, axis_index_groups=planes)


def outer_update(average, global_prev, momentum, local):
    new_momentum = MOMENTUM * momentum + average
    new_global = global_prev - OUTER_RATE * (MOMENTUM * new_momentum + average)
    merged = (MIXING * local.astype(jnp.float32) + (1.0 - MIXING) * new_global).astype(jnp.bfloat16)
    return new_global, new_momentum, merged[None]


def body(hidden, lengths, ranks, gain, head, local_frag, global_prev, momentum):
    barrier = lax.optimization_barrier
    replicas = lax.axis_size("rep")
    here = lax.axis_index("fsdp")
    core, place = here % 2, here // 2
    gain_wide, head_wide = gain.astype(jnp.float32)[None], head.astype(jnp.float32)[None]
    local = local_frag[0]

    mine = outer_reduce(local)

    own = gain_wide * head_wide
    twin = along(own, 1)
    pair = jnp.where(core == 0, jnp.concatenate([own, twin], 1), jnp.concatenate([twin, own], 1))
    blocks = (pair, along(pair, 2), along(pair, 4), along(pair, 6))

    mine, blocks = barrier((mine, blocks))
    partial = jnp.sum(mine.astype(jnp.float32), axis=0)
    partial, blocks = barrier((partial, blocks))
    far = lax.ppermute(partial, "rep", [(i, (i + PLANE) % replicas) for i in range(replicas)])

    w, alpha, beta, v = score_call(place.astype(jnp.int32).reshape(1, 1), lengths, ranks, hidden, blocks)
    far, w, alpha, beta, v = barrier((far, w, alpha, beta, v))

    sent, spread = outer_spread(outer_average(partial + far, global_prev))
    sent, w, alpha = barrier((sent, w, alpha))
    average = spread(sent)

    w = w[0:1] + along(w[1:2], 2) + along(w[2:3], 4) + along(w[3:4], 6)
    half = own.shape[1]
    low, high = w[:, :half], w[:, half:]
    w = jnp.where(core == 0, low, high) + along(jnp.where(core == 0, high, low), 1)
    d_hidden = token_call(hidden, v, alpha, beta)

    new_global, new_momentum, merged = outer_update(
        average.reshape(global_prev.shape).astype(jnp.float32), global_prev, momentum, local
    )
    return d_hidden, w * head_wide, w * gain_wide, new_global, new_momentum, merged


def solution(mesh):
    placed = (
        P(("rep", "fsdp"), None),
        P(("rep", "fsdp"), None),
        P(("rep", "fsdp"), None),
        P("fsdp"),
        P("fsdp"),
        P("rep", "fsdp", None),
        P("fsdp", None),
        P("fsdp", None),
    )
    return jax.shard_map(
        body,
        mesh=mesh,
        in_specs=placed,
        out_specs=(
            P(("rep", "fsdp"), None),
            P("rep", "fsdp"),
            P("rep", "fsdp"),
            P("fsdp", None),
            P("fsdp", None),
            P("rep", "fsdp", None),
        ),
        check_vma=False,
    )
```

time: 82 us -> 59.8 us (0.73)
  the two profiles are of different devices: /device:TPU:1 before, /device:TPU:2 now
where the time goes in v2:
time: 59.8 us; the launch traced here: 59.4 us
  starting transfers between devices  30.7 us (51%)
  waiting for transfers between devices  10.5 us (18%)
  Pallas kernels  6.81 us (11%)
  other arithmetic  6.37 us (11%)
  local copies, waits for them, and re-layouts  4.22 us (7%)
  between operations  0.81 us (1%)
    ppermute x8, starting transfers between devices, along(): return lax.ppermute(array, 'fsdp', [(i, i ^ k) for i in range(devices)])  9.84 us
    all_to_all x1, starting transfers between devices, outer_reduce(): lax.all_to_all(local.reshape(PLANE, rows // PLANE, width), 'rep', 0, 0, t...  7.61 us
    all_to_all x1, starting transfers between devices, outer_spread(): lax.all_to_all(sent, 'rep', 0, 0, tiled=True, axis_index_groups=planes)  7.09 us
    ppermute x8, waiting for transfers between devices, along(): return lax.ppermute(array, 'fsdp', [(i, i ^ k) for i in range(devices)])  6.55 us
    ppermute x1, starting transfers between devices, body(): lax.ppermute(partial, 'rep', [(i, (i + PLANE) % replicas) for i in range(...  6.13 us
    all_to_all x1, waiting for transfers between devices, outer_spread(): lax.all_to_all(sent, 'rep', 0, 0, tiled=True, axis_index_groups=planes)  3.99 us
    pallas_call x1, Pallas kernels, token_call(): pl.pallas_call(token_kernel, grid=(tokens // step,), out_shape=jax.ShapeD...  3.71 us
    broadcast_in_dim x1, other arithmetic, outer_update(): return (new_global, new_momentum, merged[None])  3.55 us
  transfers between devices with their start and end apart: 11, of which 4 were waited for; matrix products, arithmetic and copies ran while one was open for 2% of the time, Pallas kernels for 11%

profile of v2, /device:TPU:2, one launch (start us, length us, event | category | flops | bytes accessed | tf_op | source)
XLA Modules:
  0.0 59.4 jit_solution(8855487052838228141)
XLA Ops:
  0.6 0.0 copy-start.5
  0.6 0.0 copy-start.4
  0.7 0.0 copy-start
  0.7 2.2 %reshape_squeeze.3 = bf16[16,4,4608]{2,1,0:T(4,128)(2,1)} reshape(bf16[1,64,4608]{2,1,0:T(8,128)(2,1)} %param.13) | data formatting | bytes 1179648 | tf_op jit(solution)/shard_map/reshape;squeeze | solution.py:146
  2.8 0.0 copy-start.1
  2.8 0.0 copy-start.2
  2.8 7.6 %all-to-all-start = ((bf16[16,4,4608]{2,1,0:T(4,128)(2,1)}), bf16[16,4,4608]{2,1,0:T(4,128)(2,1)S(1)}, u32[]{:S(2)}, u32[]{:S(2)}) async-start(bf16[16,4,4608]{2,1,0:T(4,128)(2,1)} %reshape_squeeze.3), calls=%async_computation | async-start | bytes 1179648 | tf_op jit(solution)/shard_map/all_to_all | solution.py:145
  10.4 0.0 copy-done.5
  10.4 0.0 copy-done.4
  10.5 0.1 collective-permute-start
  10.6 1.1 %collective-permute-done = f32[1,576]{1,0:T(1,128)S(1)} collective-permute-done((f32[1,576]{1,0:T(1,128)S(1)}, f32[1,576]{1,0:T(1,128)S(1)}, u32[]{:S(2)}, u32[]{:S(2)}) %collective-permute-start) | collective-permute-done | bytes 2336 | tf_op jit(solution)/shard_map/ppermute | solution.py:139
  11.7 0.1 broadcast_select_fusion.own_ref
  11.8 2.0 %collective-permute-start.1 = (f32[1,1152]{1,0:T(1,128)S(1)}, f32[1,1152]{1,0:T(1,128)S(1)}, u32[]{:S(2)}, u32[]{:S(2)}) collective-permute-start(f32[1,1152]{1,0:T(1,128)S(1)} %broadcast_select_fusion.own_ref), channel_id=1, source_target_pairs={{0,2},{1,3},{2,0},{3,1},{4,6},{5,7},{6,4},{7,5},{8,10},{9,11},{10,... | collective-permute-start | bytes 13832 | tf_op jit(solution)/shard_map/ppermute | solution.py:139
  13.8 3.3 %collective-permute-start.2 = (f32[1,1152]{1,0:T(1,128)S(1)}, f32[1,1152]{1,0:T(1,128)S(1)}, u32[]{:S(2)}, u32[]{:S(2)}) collective-permute-start(f32[1,1152]{1,0:T(1,128)S(1)} %broadcast_select_fusion.own_ref), channel_id=1, source_target_pairs={{0,4},{1,5},{2,6},{3,7},{4,0},{5,1},{6,2},{7,3},{8,12},{9,13},{10,... | collective-permute-start | bytes 13832 | tf_op jit(solution)/shard_map/ppermute | solution.py:139
  17.0 0.0 collective-permute-start.3
  17.0 0.0 collective-permute-done.1.one_ref
  17.0 1.6 %collective-permute-done.2.two_ref = f32[1,1152]{1,0:T(1,128)S(1)} collective-permute-done((f32[1,1152]{1,0:T(1,128)S(1)}, f32[1,1152]{1,0:T(1,128)S(1)}, u32[]{:S(2)}, u32[]{:S(2)}) %collective-permute-start.2) | collective-permute-done | bytes 4640 | tf_op jit(solution)/shard_map/ppermute | solution.py:139
  18.6 3.8 %collective-permute-done.3.three_ref = f32[1,1152]{1,0:T(1,128)S(1)} collective-permute-done((f32[1,1152]{1,0:T(1,128)S(1)}, f32[1,1152]{1,0:T(1,128)S(1)}, u32[]{:S(2)}, u32[]{:S(2)}) %collective-permute-start.3) | collective-permute-done | bytes 4640 | tf_op jit(solution)/shard_map/ppermute | solution.py:139
  22.4 0.0 all-to-all-done
  22.5 0.2 convert_reduce_fusion
  22.7 6.1 %collective-permute-start.4 = (f32[4,4608]{1,0:T(4,128)S(1)}, f32[4,4608]{1,0:T(4,128)S(1)}, u32[]{:S(2)}, u32[]{:S(2)}) collective-permute-start(f32[4,4608]{1,0:T(4,128)S(1)} %convert_reduce_fusion), channel_id=1, source_target_pairs={{0,128},{8,136},{16,144},{24,152},{32,160},{40,168},{48,176},{56,1... | collective-permute-start | bytes 221192 | tf_op jit(solution)/shard_map/ppermute | solution.py:187
  28.8 0.0 copy-done
  28.8 0.0 copy-done.1
  28.8 0.0 copy-done.2
  28.8 3.1 %score.1 = (f32[4,1152]{1,0:T(4,128)S(1)}, f32[256,1]{1,0:T(8,128)S(1)}, f32[256,1]{1,0:T(8,128)S(1)}, f32[1,4608]{1,0:T(1,128)S(1)}) custom-call(s32[1,1]{1,0:T(1,128)} %bitcast.place_ref, s32[1,8]{1,0:T(1,128)S(1)} %copy-done.1, s32[1,8]{1,0:T(1,128)S(1)} %copy-done.2, bf16[256,4608]{1,0:T(8,128)(2,1)S(1)} %copy-done, ...), custom_call_target="tpu_custom_call" | custom-call | flops 7077888 | bytes 2359296 | tf_op jit(solution)/shard_map/score/pallas_call | solution.py:97
  31.9 0.0 collective-permute-done.4
  32.0 1.0 %subtract_convert_fusion = f16[4,4608]{1,0:T(4,128)(2,1)S(1)} fusion(f32[4,4608]{1,0:T(4,128)S(1)} %convert_reduce_fusion, f32[4,4608]{1,0:T(4,128)S(1)} %collective-permute-done.4, f32[64,4608]{1,0:T(8,128)} %param.14, s32[]{:T(128)S(6)} %select_n.46), kind=kLoop, calls=%fused_computation.7 | loop fusion | flops 73728 | bytes 258052 | tf_op jit(solution)/shard_map/convert_element_type | solution.py:158
  32.9 1.0 %broadcast_in_dim.15 = f16[16,4,4608]{2,1,0:T(4,128)(2,1)} broadcast(f16[4,4608]{1,0:T(4,128)(2,1)S(1)} %subtract_convert_fusion), dimensions={1,2} | broadcast | bytes 626688 | tf_op jit(solution)/shard_map/broadcast_in_dim | solution.py:158
  33.9 3.4 %collective-permute-start.7 = (f32[1,1152]{1,0:T(1,128)S(1)}, f32[1,1152]{1,0:T(1,128)S(1)}, u32[]{:S(2)}, u32[]{:S(2)}) collective-permute-start(f32[1,1152]{1,0:T(1,128)S(1)} %get-tuple-element.56), channel_id=1, source_target_pairs={{0,6},{1,7},{2,4},{3,5},{4,2},{5,3},{6,0},{7,1},{8,14},{9,15},{10,... | collective-permute-start | bytes 13832 | tf_op jit(solution)/shard_map/ppermute | solution.py:139
  37.3 0.0 collective-permute-start.6
  37.3 1.0 %collective-permute-start.5 = (f32[1,1152]{1,0:T(1,128)S(1)}, f32[1,1152]{1,0:T(1,128)S(1)}, u32[]{:S(2)}, u32[]{:S(2)}) collective-permute-start(f32[1,1152]{1,0:T(1,128)S(1)} %get-tuple-element.55), channel_id=1, source_target_pairs={{0,2},{1,3},{2,0},{3,1},{4,6},{5,7},{6,4},{7,5},{8,10},{9,11},{10,... | collective-permute-start | bytes 13832 | tf_op jit(solution)/shard_map/ppermute | solution.py:139
  38.4 7.1 %all-to-all-start.1 = ((f16[16,4,4608]{2,1,0:T(4,128)(2,1)}), f16[16,4,4608]{2,1,0:T(4,128)(2,1)S(1)}, u32[]{:S(2)}, u32[]{:S(2)}) async-start(f16[16,4,4608]{2,1,0:T(4,128)(2,1)} %broadcast_in_dim.15), calls=%async_computation.1 | async-start | bytes 1179648 | tf_op jit(solution)/shard_map/all_to_all | solution.py:159
  45.5 0.0 collective-permute-done.7
  45.5 0.0 collective-permute-done.6
  45.5 0.0 collective-permute-done.5
  45.5 0.1 broadcast_select_fusion.1
  45.6 0.0 collective-permute-start.8
  45.7 3.7 %token_grad.1 = bf16[256,4608]{1,0:T(8,128)(2,1)} custom-call(bf16[256,4608]{1,0:T(8,128)(2,1)S(1)} %copy-done, f32[1,4608]{1,0:T(1,128)S(1)} %get-tuple-element.42.v_ref, f32[256,1]{1,0:T(8,128)S(1)} %get-tuple-element.46.alpha_ref, f32[256,1]{1,0:T(8,128)S(1)} %get-tuple-element.47.beta_ref), custom_call_target="tpu_custom_call" | custom-call | flops 4718592 | bytes 4718592 | tf_op jit(solution)/shard_map/token_grad/pallas_call | solution.py:120
  49.4 0.0 collective-permute-done.8
  49.4 0.7 %reshape_multiply_fusion = (f32[1,576]{1,0:T(1,128)}, f32[1,576]{1,0:T(1,128)S(1)}) fusion(f32[576]{0:T(1024)S(1)} %convert_element_type.27, f32[1,576]{1,0:T(1,128)S(1)} %collective-permute-done.8, f32[1,1152]{1,0:T(1,128)S(1)} %add_add_fusion, pred[]{:T(512)S(6)} %eq.4), kind=kLoop, calls=%fused_computation.13 | loop fusion | flops 1728 | bytes 13825 | tf_op jit(solution)/shard_map/mul | solution.py:205
  50.0 0.6 reshape_multiply_fusion.1
  50.6 4.0 %all-to-all-done.1 = f16[16,4,4608]{2,1,0:T(4,128)(2,1)S(1)} async-done(((f16[16,4,4608]{2,1,0:T(4,128)(2,1)}), f16[16,4,4608]{2,1,0:T(4,128)(2,1)S(1)}, u32[]{:S(2)}, u32[]{:S(2)}) %all-to-all-start.1) | async-done | bytes 589856 | tf_op jit(solution)/shard_map/all_to_all | solution.py:159
  54.6 0.2 convert_element_type.36
  54.8 0.0 copy-start.3
  54.8 0.4 reshape.83
  55.2 0.6 %copy-done.3 = bf16[1,64,4608]{2,1,0:T(8,128)(2,1)S(1)} copy-done((bf16[1,64,4608]{2,1,0:T(8,128)(2,1)S(1)}, bf16[1,64,4608]{2,1,0:T(8,128)(2,1)}, u32[]{:S(2)}) %copy-start.3) | copy-done | bytes 589848
  55.9 3.5 %fusion.2 = (bf16[1,64,4608]{2,1,0:T(8,128)(2,1)}, f32[64,4608]{1,0:T(8,128)}, f32[64,4608]{1,0:T(8,128)}) fusion(bf16[1,64,4608]{2,1,0:T(8,128)(2,1)S(1)} %copy-done.3, f32[64,4608]{1,0:T(8,128)} %param.14, f32[64,4608]{1,0:T(8,128)S(1)} %reshape.83, f32[64,4608]{1,0:T(8,128)} %param.15), kind=kLoop, calls=%fused_computation.6 | loop fusion | flops 2949120 | bytes 7077888 | tf_op jit(solution)/shard_map/broadcast_in_dim | solution.py:166
  (6 shorter events, 0.0 us)
Async XLA Ops:
  0.6 9.8 %copy-start.5 = (bf16[576]{0:T(1024)(128)(2,1)S(1)}, bf16[576]{0:T(1024)(128)(2,1)}, u32[]{:S(2)}) copy-start(bf16[576]{0:T(1024)(128)(2,1)} %param.12) | copy-start | bytes 3460
  0.6 9.8 %copy-start.4 = (bf16[576]{0:T(1024)(128)(2,1)S(1)}, bf16[576]{0:T(1024)(128)(2,1)}, u32[]{:S(2)}) copy-start(bf16[576]{0:T(1024)(128)(2,1)} %param.11) | copy-start | bytes 3460
  0.7 28.2 %copy-start = (bf16[256,4608]{1,0:T(8,128)(2,1)S(1)}, bf16[256,4608]{1,0:T(8,128)(2,1)}, u32[]{:S(2)}) copy-start(bf16[256,4608]{1,0:T(8,128)(2,1)} %hidden_ref.3) | copy-start | bytes 7077892
  2.8 26.0 %copy-start.1 = (s32[1,8]{1,0:T(1,128)S(1)}, s32[1,8]{1,0:T(1,128)}, u32[]{:S(2)}) copy-start(s32[1,8]{1,0:T(1,128)} %lengths_ref.1) | copy-start | bytes 100
  2.8 26.0 %copy-start.2 = (s32[1,8]{1,0:T(1,128)S(1)}, s32[1,8]{1,0:T(1,128)}, u32[]{:S(2)}) copy-start(s32[1,8]{1,0:T(1,128)} %ranks_ref.1) | copy-start | bytes 100
  2.8 19.6 %all-to-all-start = ((bf16[16,4,4608]{2,1,0:T(4,128)(2,1)}), bf16[16,4,4608]{2,1,0:T(4,128)(2,1)S(1)}, u32[]{:S(2)}, u32[]{:S(2)}) async-start(bf16[16,4,4608]{2,1,0:T(4,128)(2,1)} %reshape_squeeze.3), calls=%async_computation | async-start | bytes 1179648 | tf_op jit(solution)/shard_map/all_to_all | solution.py:145
  10.5 1.2 %collective-permute-start = (f32[1,576]{1,0:T(1,128)S(1)}, f32[1,576]{1,0:T(1,128)S(1)}, u32[]{:S(2)}, u32[]{:S(2)}) collective-permute-start(f32[1,576]{1,0:T(1,128)S(1)} %concatenate.24), channel_id=1, source_target_pairs={{0,1},{1,0},{2,3},{3,2},{4,5},{5,4},{6,7},{7,6},{8,9},{9,8},{10,11... | collective-permute-start | bytes 6920 | tf_op jit(solution)/shard_map/ppermute | solution.py:139
  11.8 5.2 %collective-permute-start.1 = (f32[1,1152]{1,0:T(1,128)S(1)}, f32[1,1152]{1,0:T(1,128)S(1)}, u32[]{:S(2)}, u32[]{:S(2)}) collective-permute-start(f32[1,1152]{1,0:T(1,128)S(1)} %broadcast_select_fusion.own_ref), channel_id=1, source_target_pairs={{0,2},{1,3},{2,0},{3,1},{4,6},{5,7},{6,4},{7,5},{8,10},{9,11},{10,... | collective-permute-start | bytes 13832 | tf_op jit(solution)/shard_map/ppermute | solution.py:139
  13.8 4.9 %collective-permute-start.2 = (f32[1,1152]{1,0:T(1,128)S(1)}, f32[1,1152]{1,0:T(1,128)S(1)}, u32[]{:S(2)}, u32[]{:S(2)}) collective-permute-start(f32[1,1152]{1,0:T(1,128)S(1)} %broadcast_select_fusion.own_ref), channel_id=1, source_target_pairs={{0,4},{1,5},{2,6},{3,7},{4,0},{5,1},{6,2},{7,3},{8,12},{9,13},{10,... | collective-permute-start | bytes 13832 | tf_op jit(solution)/shard_map/ppermute | solution.py:139
  17.0 5.4 %collective-permute-start.3 = (f32[1,1152]{1,0:T(1,128)S(1)}, f32[1,1152]{1,0:T(1,128)S(1)}, u32[]{:S(2)}, u32[]{:S(2)}) collective-permute-start(f32[1,1152]{1,0:T(1,128)S(1)} %broadcast_select_fusion.own_ref), channel_id=1, source_target_pairs={{0,6},{1,7},{2,4},{3,5},{4,2},{5,3},{6,0},{7,1},{8,14},{9,15},{10,... | collective-permute-start | bytes 13832 | tf_op jit(solution)/shard_map/ppermute | solution.py:139
  22.7 9.3 %collective-permute-start.4 = (f32[4,4608]{1,0:T(4,128)S(1)}, f32[4,4608]{1,0:T(4,128)S(1)}, u32[]{:S(2)}, u32[]{:S(2)}) collective-permute-start(f32[4,4608]{1,0:T(4,128)S(1)} %convert_reduce_fusion), channel_id=1, source_target_pairs={{0,128},{8,136},{16,144},{24,152},{32,160},{40,168},{48,176},{56,1... | collective-permute-start | bytes 221192 | tf_op jit(solution)/shard_map/ppermute | solution.py:187
  33.9 11.6 %collective-permute-start.7 = (f32[1,1152]{1,0:T(1,128)S(1)}, f32[1,1152]{1,0:T(1,128)S(1)}, u32[]{:S(2)}, u32[]{:S(2)}) collective-permute-start(f32[1,1152]{1,0:T(1,128)S(1)} %get-tuple-element.56), channel_id=1, source_target_pairs={{0,6},{1,7},{2,4},{3,5},{4,2},{5,3},{6,0},{7,1},{8,14},{9,15},{10,... | collective-permute-start | bytes 13832 | tf_op jit(solution)/shard_map/ppermute | solution.py:139
  37.3 8.1 %collective-permute-start.6 = (f32[1,1152]{1,0:T(1,128)S(1)}, f32[1,1152]{1,0:T(1,128)S(1)}, u32[]{:S(2)}, u32[]{:S(2)}) collective-permute-start(f32[1,1152]{1,0:T(1,128)S(1)} %get-tuple-element.57), channel_id=1, source_target_pairs={{0,4},{1,5},{2,6},{3,7},{4,0},{5,1},{6,2},{7,3},{8,12},{9,13},{10,... | collective-permute-start | bytes 13832 | tf_op jit(solution)/shard_map/ppermute | solution.py:139
  37.3 8.1 %collective-permute-start.5 = (f32[1,1152]{1,0:T(1,128)S(1)}, f32[1,1152]{1,0:T(1,128)S(1)}, u32[]{:S(2)}, u32[]{:S(2)}) collective-permute-start(f32[1,1152]{1,0:T(1,128)S(1)} %get-tuple-element.55), channel_id=1, source_target_pairs={{0,2},{1,3},{2,0},{3,1},{4,6},{5,7},{6,4},{7,5},{8,10},{9,11},{10,... | collective-permute-start | bytes 13832 | tf_op jit(solution)/shard_map/ppermute | solution.py:139
  38.4 16.2 %all-to-all-start.1 = ((f16[16,4,4608]{2,1,0:T(4,128)(2,1)}), f16[16,4,4608]{2,1,0:T(4,128)(2,1)S(1)}, u32[]{:S(2)}, u32[]{:S(2)}) async-start(f16[16,4,4608]{2,1,0:T(4,128)(2,1)} %broadcast_in_dim.15), calls=%async_computation.1 | async-start | bytes 1179648 | tf_op jit(solution)/shard_map/all_to_all | solution.py:159
  45.6 3.8 %collective-permute-start.8 = (f32[1,576]{1,0:T(1,128)S(1)}, f32[1,576]{1,0:T(1,128)S(1)}, u32[]{:S(2)}, u32[]{:S(2)}) collective-permute-start(f32[1,576]{1,0:T(1,128)S(1)} %broadcast_select_fusion.1), channel_id=1, source_target_pairs={{0,1},{1,0},{2,3},{3,2},{4,5},{5,4},{6,7},{7,6},{8,9},{9,8},{10,11... | collective-permute-start | bytes 6920 | tf_op jit(solution)/shard_map/ppermute | solution.py:139
  54.8 1.1 %copy-start.3 = (bf16[1,64,4608]{2,1,0:T(8,128)(2,1)S(1)}, bf16[1,64,4608]{2,1,0:T(8,128)(2,1)}, u32[]{:S(2)}) copy-start(bf16[1,64,4608]{2,1,0:T(8,128)(2,1)} %param.13) | copy-start | bytes 1769476

commit v3 on v1

v3 whole, which is shorter than its diff:
```python
import jax
import jax.numpy as jnp
from jax import lax
from jax.experimental import pallas as pl
from jax.experimental.pallas import tpu as pltpu
from jax.sharding import PartitionSpec as P

LIST_LEN = 256
CAND = 8
LANES = 128
ROWS = 32

SOFTCAP = 30.0
TEMPER = 2.0
LOSS_SCALE = 512.0
OUTER_RATE = 0.7
MOMENTUM = 0.9
MIXING = 0.5
EPSILON = 1e-06

PLANES = 2
PLANE = 16
TALL, BROAD = 16, 1152
LARGEST = 10.0
STEPS = 32767.0
SHARES = 4
VMEM_LIMIT = 16 * 1024 * 1024


def score_kernel(lengths_ref, ranks_ref, hidden_ref, v_ref, alpha_ref, beta_ref, square_ref, dot_ref):
    tokens, width = hidden_ref.shape

    def first(step, carry):
        rows = pl.ds(pl.multiple_of(step * ROWS, ROWS), ROWS)
        square = jnp.zeros((ROWS, LANES), jnp.float32)
        dot = jnp.zeros((ROWS, LANES), jnp.float32)
        for j in range(width // LANES):
            part = slice(j * LANES, (j + 1) * LANES)
            values = hidden_ref[rows, part].astype(jnp.float32)
            square += values * values
            dot += values * v_ref[:, part]
        square_ref[rows, :] = jnp.sum(square, axis=1, keepdims=True)
        dot_ref[rows, :] = jnp.sum(dot, axis=1, keepdims=True)
        return carry

    lax.fori_loop(0, tokens // ROWS, first, 0)

    inverse = lax.rsqrt(square_ref[...] / width + EPSILON)
    dots = dot_ref[...]

    lane = lax.broadcasted_iota(jnp.int32, (1, LANES), 1)
    starts = jnp.zeros((1, LANES), jnp.int32)
    ends = jnp.zeros((1, LANES), jnp.int32)
    ranks = jnp.zeros((1, LANES), jnp.int32)
    end = jnp.int32(0)
    for c in range(CAND):
        start, end = end, end + lengths_ref[0, c]
        starts = jnp.where(lane == c, start, starts)
        ends = jnp.where(lane == c, end, ends)
        ranks = jnp.where(lane == c, ranks_ref[0, c], ranks)
    real = lane < CAND
    root = jnp.sqrt(jnp.where(real, ends - starts, 1).astype(jnp.float32))
    position = lax.broadcasted_iota(jnp.int32, (tokens, LANES), 0)
    member = (position >= starts) & (position < ends)

    raw = jnp.sum(jnp.where(member, inverse * dots, 0.0), axis=0, keepdims=True) / root
    capped = SOFTCAP * jnp.tanh(raw / SOFTCAP)
    weights = jnp.where(real, jnp.exp(capped), 0.0)
    probs = weights / jnp.sum(weights, axis=1, keepdims=True)
    teacher = jnp.where(real, jnp.exp(-ranks.astype(jnp.float32) / TEMPER), 0.0)
    target = teacher / jnp.sum(teacher, axis=1, keepdims=True)
    slope = LOSS_SCALE * (probs - target) * (1.0 - (capped / SOFTCAP) ** 2)
    scale = jnp.sum(jnp.where(member, slope / root, 0.0), axis=1, keepdims=True)

    alpha = inverse * scale
    alpha_ref[...] = jnp.broadcast_to(alpha, alpha_ref.shape)
    beta_ref[...] = jnp.broadcast_to(alpha * inverse * inverse * dots / width, beta_ref.shape)


def score_call(lengths, ranks, hidden, v):
    tokens, width = hidden.shape
    smem = pl.BlockSpec(memory_space=pltpu.SMEM)
    vmem = pl.BlockSpec(memory_space=pltpu.VMEM)
    wide = jax.ShapeDtypeStruct((tokens, LANES), jnp.float32)
    return pl.pallas_call(
        score_kernel,
        out_shape=(wide, wide),
        in_specs=[smem, smem, vmem, vmem],
        out_specs=(vmem, vmem),
        scratch_shapes=[pltpu.VMEM((tokens, 1), jnp.float32)] * 2,
        compiler_params=pltpu.CompilerParams(vmem_limit_bytes=VMEM_LIMIT),
        cost_estimate=pl.CostEstimate(flops=4 * tokens * width, bytes_accessed=2 * tokens * width, transcendentals=0),
        name="score",
    )(lengths, ranks, hidden, v)


def weigh_kernel(hidden_ref, alpha_ref, mark_ref, w_ref):
    tokens, width = hidden_ref.shape
    for j in range(width // LANES):
        part = slice(j * LANES, (j + 1) * LANES)
        total = jnp.zeros((ROWS, LANES), jnp.float32)
        for row in range(0, tokens, ROWS):
            rows = slice(row, row + ROWS)
            total += alpha_ref[rows, :] * hidden_ref[rows, part].astype(jnp.float32)
        w_ref[:, part] = jnp.sum(total, axis=0, keepdims=True) * (1.0 / LOSS_SCALE)


def weigh_call(hidden, alpha, mark):
    tokens, width = hidden.shape
    vmem = pl.BlockSpec(memory_space=pltpu.VMEM)
    return pl.pallas_call(
        weigh_kernel,
        out_shape=jax.ShapeDtypeStruct((1, width), jnp.float32),
        in_specs=[vmem] * 3,
        out_specs=vmem,
        compiler_params=pltpu.CompilerParams(vmem_limit_bytes=VMEM_LIMIT),
        cost_estimate=pl.CostEstimate(flops=2 * tokens * width, bytes_accessed=2 * tokens * width, transcendentals=0),
        name="weigh",
    )(hidden, alpha, mark)


def token_kernel(hidden_ref, v_ref, alpha_ref, beta_ref, out_ref, kept_ref, sem):
    tokens, width = hidden_ref.shape
    copies = []
    for band in range(width // BROAD):
        for j in range(BROAD // LANES):
            part = slice(band * BROAD + j * LANES, band * BROAD + (j + 1) * LANES)
            v = v_ref[:, part]
            for row in range(0, tokens, ROWS):
                rows = slice(row, row + ROWS)
                values = hidden_ref[rows, part].astype(jnp.float32)
                kept_ref[rows, part] = (alpha_ref[rows, :] * v - beta_ref[rows, :] * values).astype(kept_ref.dtype)
        columns = slice(band * BROAD, (band + 1) * BROAD)
        copies.append(pltpu.make_async_copy(kept_ref.at[:, columns], out_ref.at[:, columns], sem.at[band]))
        copies[-1].start()
    for copy in copies:
        copy.wait()


def token_call(hidden, v, alpha, beta):
    tokens, width = hidden.shape
    vmem = pl.BlockSpec(memory_space=pltpu.VMEM)
    return pl.pallas_call(
        token_kernel,
        out_shape=jax.ShapeDtypeStruct((tokens, width), jnp.bfloat16),
        in_specs=[vmem] * 4,
        out_specs=pl.BlockSpec(memory_space=pl.ANY),
        scratch_shapes=[pltpu.VMEM((tokens, width), jnp.bfloat16), pltpu.SemaphoreType.DMA((width // BROAD,))],
        compiler_params=pltpu.CompilerParams(vmem_limit_bytes=VMEM_LIMIT),
        cost_estimate=pl.CostEstimate(flops=6 * tokens * width, bytes_accessed=4 * tokens * width, transcendentals=0),
        name="token_grad",
    )(hidden, v, alpha, beta)


def along(array, k):
    devices = lax.axis_size("fsdp")
    return lax.ppermute(array, "fsdp", [(i, i ^ k) for i in range(devices)])


def average_kernel(near_ref, far_ref, global_ref, out_ref, mark_ref, coded_ref, sem):
    average = global_ref[...] - (near_ref[...] + far_ref[...]) * (1.0 / (PLANES * PLANE))
    top = jnp.max(jnp.abs(average), axis=1, keepdims=True)
    unit = jnp.clip(jnp.ceil(top * (STEPS / LARGEST)), 1.0, STEPS)
    steps = jnp.clip(jnp.floor(average * ((STEPS * STEPS / LARGEST) / unit) + 0.5), -STEPS, STEPS)
    copies = []
    for part in range(SHARES):
        coded_ref[part, :, :BROAD] = steps.astype(jnp.int32).astype(coded_ref.dtype)
        coded_ref[part, :, BROAD:] = jnp.broadcast_to(unit, (TALL, LANES)).astype(jnp.int32).astype(coded_ref.dtype)
    for part in range(PLANE // SHARES):
        copies.append(pltpu.make_async_copy(coded_ref, out_ref.at[pl.ds(part * SHARES, SHARES)], sem.at[part]))
    mark_ref[...] = jnp.zeros_like(mark_ref)
    for copy in copies:
        copy.start()
    for copy in copies:
        copy.wait()


def average_call(near, far, own_global):
    vmem = pl.BlockSpec(memory_space=pltpu.VMEM)
    return pl.pallas_call(
        average_kernel,
        out_shape=(jax.ShapeDtypeStruct((PLANE, TALL, BROAD + LANES), jnp.int16), jax.ShapeDtypeStruct((1, LANES), jnp.float32)),
        in_specs=[vmem, vmem, vmem],
        out_specs=(pl.BlockSpec(memory_space=pl.ANY), vmem),
        scratch_shapes=[pltpu.VMEM((SHARES, TALL, BROAD + LANES), jnp.int16), pltpu.SemaphoreType.DMA((PLANE // SHARES,))],
        compiler_params=pltpu.CompilerParams(vmem_limit_bytes=VMEM_LIMIT),
        cost_estimate=pl.CostEstimate(flops=10 * near.size, bytes_accessed=40 * near.size, transcendentals=0),
        name="average",
    )(near, far, own_global)


def update_kernel(coded_ref, w_ref, gain_ref, head_ref, global_ref, momentum_ref, local_ref,
                  grad_gain_ref, grad_head_ref, *refs):
    outs, kept, sem = refs[:3], refs[3:6], refs[6]
    rows, width = global_ref.shape
    across = width // BROAD
    new_global_ref, new_momentum_ref, merged_ref = kept
    copies = []
    for band in range(rows // TALL):
        row = slice(band * TALL, (band + 1) * TALL)
        for column in range(across):
            p = band * across + column
            scale = coded_ref[p, :, BROAD:].astype(jnp.int32).astype(jnp.float32) * (LARGEST / (STEPS * STEPS))
            for j in range(BROAD // LANES):
                part = slice(column * BROAD + j * LANES, column * BROAD + (j + 1) * LANES)
                steps = coded_ref[p, :, j * LANES:(j + 1) * LANES].astype(jnp.int32).astype(jnp.float32)
                average = steps * scale
                new_momentum = MOMENTUM * momentum_ref[row, part] + average
                new_global = global_ref[row, part] - OUTER_RATE * (MOMENTUM * new_momentum + average)
                new_momentum_ref[row, part] = new_momentum
                new_global_ref[row, part] = new_global
                merged = MIXING * local_ref[row, part].astype(jnp.float32) + (1.0 - MIXING) * new_global
                merged_ref[row, part] = merged.astype(merged_ref.dtype)
        for n in range(3):
            copies.append(pltpu.make_async_copy(kept[n].at[row, :], outs[n].at[row, :], sem.at[n, band]))
            copies[-1].start()
    w = w_ref[...]
    grad_gain_ref[...] = w * head_ref[...]
    grad_head_ref[...] = w * gain_ref[...]
    for copy in copies:
        copy.wait()


def update_call(coded, w, gain, head, global_prev, momentum, local):
    rows, width = global_prev.shape
    vmem = pl.BlockSpec(memory_space=pltpu.VMEM)
    whole = pl.BlockSpec(memory_space=pl.ANY)
    wide, narrow = jnp.float32, jnp.bfloat16
    grad = jax.ShapeDtypeStruct(w.shape, wide)
    return pl.pallas_call(
        update_kernel,
        out_shape=(grad, grad) + tuple(jax.ShapeDtypeStruct((rows, width), t) for t in (wide, wide, narrow)),
        in_specs=[vmem] * 7,
        out_specs=(vmem,) * 2 + (whole,) * 3,
        scratch_shapes=[pltpu.VMEM((rows, width), t) for t in (wide, wide, narrow)]
        + [pltpu.SemaphoreType.DMA((3, rows // TALL))],
        compiler_params=pltpu.CompilerParams(vmem_limit_bytes=VMEM_LIMIT),
        cost_estimate=pl.CostEstimate(flops=10 * rows * width, bytes_accessed=22 * rows * width, transcendentals=0),
        name="update",
    )(coded, w, gain, head, global_prev, momentum, local)


def body(hidden, lengths, ranks, gain, head, local_frag, global_prev, momentum):
    barrier = lax.optimization_barrier
    replicas, devices = lax.axis_size("rep"), lax.axis_size("fsdp")
    planes = [[PLANE * z + i for i in range(PLANE)] for z in range(PLANES)]
    here = lax.axis_index("fsdp")
    local = local_frag[0]

    pieces = local.reshape(4, TALL, 4, BROAD).transpose(0, 2, 1, 3).reshape(PLANE, TALL, BROAD)
    pieces, gain, head = barrier((pieces, gain, head))
    gain_wide, head_wide = gain.astype(jnp.float32)[None], head.astype(jnp.float32)[None]
    mine = lax.all_to_all(pieces, "rep", 0, 0, tiled=True, axis_index_groups=planes)

    v = gain_wide * head_wide
    for bit in (1, 2, 4):
        other = along(v, bit)
        v = jnp.where(here & bit == 0, jnp.concatenate([v, other], 1), jnp.concatenate([other, v], 1))
    owned = lax.rem(lax.axis_index("rep"), PLANE)
    across = global_prev.shape[1] // BROAD
    own_global = lax.dynamic_slice(global_prev, (owned // across * TALL, owned % across * BROAD), (TALL, BROAD))

    mine, own_global = barrier((mine, own_global))
    near = jnp.sum(mine.astype(jnp.float32), axis=0)
    far = lax.ppermute(near, "rep", [(i, (i + PLANE) % replicas) for i in range(replicas)])

    alpha, beta = score_call(lengths, ranks, hidden, v)
    far, alpha, beta = barrier((far, alpha, beta))

    coded, mark = average_call(near, far, own_global)
    received = lax.all_to_all(coded, "rep", 0, 0, tiled=True, axis_index_groups=planes)

    def halve(hidden, v, alpha, beta, w):
        d_hidden = None
        for bit in (4, 2, 1):
            half = w.shape[1] // 2
            low, high = w[:, :half], w[:, half:]
            kept, sent = jnp.where(here & bit == 0, low, high), jnp.where(here & bit == 0, high, low)
            term = along(sent, bit)
            if bit == 4:
                d_hidden = token_call(hidden, v, alpha, beta)
                term, d_hidden = barrier((term, d_hidden))
            w = kept + term
        return d_hidden, w

    def no_halving(hidden, v, alpha, beta, w):
        return token_call(hidden, v, alpha, beta), w[:, :w.shape[1] // devices]

    w = weigh_call(hidden, alpha, mark)
    d_hidden, w = lax.cond(
        lax.axis_index("rep") < replicas, halve, no_halving, hidden, v, alpha, beta, w
    )

    grad_gain, grad_head, new_global, new_momentum, merged = update_call(
        received, w, gain_wide, head_wide, global_prev, momentum, local
    )
    return d_hidden, grad_gain, grad_head, new_global, new_momentum, merged[None]


def solution(mesh):
    placed = (
        P(("rep", "fsdp"), None),
        P(("rep", "fsdp"), None),
        P(("rep", "fsdp"), None),
        P("fsdp"),
        P("fsdp"),
        P("rep", "fsdp", None),
        P("fsdp", None),
        P("fsdp", None),
    )
    return jax.shard_map(
        body,
        mesh=mesh,
        in_specs=placed,
        out_specs=(
            P(("rep", "fsdp"), None),
            P("rep", "fsdp"),
            P("rep", "fsdp"),
            P("fsdp", None),
            P("fsdp", None),
            P("rep", "fsdp", None),
        ),
        check_vma=False,
    )
```

time: 82 us -> 55.5 us (0.68)
  blocking collectives: 18.8 us -> 0 us
  waiting for transfers between devices: 25.4 us -> 7.81 us
  starting transfers between devices: 20.1 us -> 29.8 us
  Pallas kernels: 6.15 us -> 12.6 us
  other arithmetic: 4.88 us -> 0.51 us
  local copies, waits for them, and re-layouts: 5.51 us -> 3.42 us
    all_to_all x3 -> x2, waiting for transfers between devices: 25.4 us -> 2.96 us  [the longest x1 2.96 us: body(): lax.all_to_all(pieces, 'rep', 0, 0, tiled=True, axis_index_groups=planes)]
    all_to_all x1 -> x0, blocking collectives: 18.8 us -> none  [outer_work(): lax.all_to_all(local.reshape(PLANE, piece, width), 'rep', 0, 0, tiled=Tru...]
    ppermute x1 -> x7, starting transfers between devices: 6.99 us -> 18.5 us  [the longest x6 11.5 us: along(): return lax.ppermute(array, 'fsdp', [(i, i ^ k) for i in range(devices)])]
    pallas_call x1 -> x5, Pallas kernels: 6.15 us -> 12.6 us  [the longest x1 3.66 us: score_call(): pl.pallas_call(score_kernel, out_shape=(wide, wide), in_specs=[smem, smem...]
    ppermute x1 -> x7, waiting for transfers between devices: 0.01 us -> 4.85 us  [the longest x6 4.85 us: along(): return lax.ppermute(array, 'fsdp', [(i, i ^ k) for i in range(devices)])]
    broadcast_in_dim x1 -> x0, other arithmetic: 3.55 us -> none  [outer_work(): return (new_global, new_momentum, merged[None])]
    broadcast_in_dim x4 -> x2, local copies, waits for them, and re-layouts: 2.95 us -> 0.01 us  [the longest x1 0.01 us: body(): gain.astype(jnp.float32)[None]]
    all_to_all x3 -> x2, starting transfers between devices: 13.2 us -> 11.3 us  [the longest x1 7.72 us: body(): lax.all_to_all(pieces, 'rep', 0, 0, tiled=True, axis_index_groups=planes)]
  transfers between devices with their start and end apart: 4 -> 9, of which waited for: 3 -> 5; matrix products, arithmetic and copies ran while one was open for 4% -> 1% of each run, Pallas kernels for 8% -> 17%
where the time goes in v3:
time: 55.5 us; the launch traced here: 55 us
  starting transfers between devices  29.8 us (54%)
  Pallas kernels  12.6 us (23%)
  waiting for transfers between devices  7.81 us (14%)
  local copies, waits for them, and re-layouts  3.42 us (6%)
  between operations  0.83 us (1%)
    ppermute x6, starting transfers between devices, along(): return lax.ppermute(array, 'fsdp', [(i, i ^ k) for i in range(devices)])  11.5 us
    all_to_all x1, starting transfers between devices, body(): lax.all_to_all(pieces, 'rep', 0, 0, tiled=True, axis_index_groups=planes)  7.72 us
    ppermute x1, starting transfers between devices, body(): lax.ppermute(near, 'rep', [(i, (i + PLANE) % replicas) for i in range(rep...  6.99 us
    ppermute x6, waiting for transfers between devices, along(): return lax.ppermute(array, 'fsdp', [(i, i ^ k) for i in range(devices)])  4.85 us
    pallas_call x1, Pallas kernels, score_call(): pl.pallas_call(score_kernel, out_shape=(wide, wide), in_specs=[smem, smem...  3.66 us
    all_to_all x1, starting transfers between devices, body(): lax.all_to_all(coded, 'rep', 0, 0, tiled=True, axis_index_groups=planes)  3.63 us
    pallas_call x1, Pallas kernels, token_call(): pl.pallas_call(token_kernel, out_shape=jax.ShapeDtypeStruct((tokens, widt...  3.36 us
    all_to_all x1, waiting for transfers between devices, body(): lax.all_to_all(pieces, 'rep', 0, 0, tiled=True, axis_index_groups=planes)  2.96 us
  transfers between devices with their start and end apart: 9, of which 5 were waited for; matrix products, arithmetic and copies ran while one was open for 1% of the time, Pallas kernels for 17%

profile of v3, /device:TPU:1, one launch (start us, length us, event | category | flops | bytes accessed | tf_op | source)
XLA Modules:
  0.0 55.0 jit_solution(7217676353788038545)
XLA Ops:
  0.6 1.2 %reshape_squeeze.3 = bf16[4,16,4,1152]{3,2,1,0:T(4,128)(2,1)S(1)} reshape(bf16[1,64,4608]{2,1,0:T(8,128)(2,1)} %param.15) | data formatting | bytes 1179648 | tf_op jit(solution)/shard_map/reshape;squeeze | solution.py:250
  1.8 0.0 copy-start.5
  1.9 0.0 copy-start.6
  1.9 0.0 copy-start.1
  1.9 0.9 %copy.14 = bf16[4,4,16,1152]{3,2,1,0:T(8,128)(2,1)} copy(bf16[4,4,16,1152]{3,1,2,0:T(4,128)(2,1)S(1)} %bitcast.5) | data formatting | bytes 1179648 | tf_op jit(solution)/shard_map/transpose | solution.py:250
  2.8 0.0 copy-start.3
  2.8 0.0 copy-start.4
  2.8 7.7 %all-to-all-start = ((bf16[16,16,1152]{2,1,0:T(8,128)(2,1)}), bf16[16,16,1152]{2,1,0:T(8,128)(2,1)S(1)}, u32[]{:S(2)}, u32[]{:S(2)}) async-start(bf16[16,16,1152]{2,1,0:T(8,128)(2,1)} %bitcast.1), calls=%async_computation | async-start | bytes 1179648 | tf_op jit(solution)/shard_map/all_to_all | solution.py:253
  10.5 0.0 copy-done.5
  10.5 0.0 copy-done.6
  10.5 1.0 %collective-permute-start.3 = (f32[1,576]{1,0:T(1,128)S(1)}, f32[1,576]{1,0:T(1,128)S(1)}, u32[]{:S(2)}, u32[]{:S(2)}) collective-permute-start(f32[1,576]{1,0:T(1,128)S(1)} %mul.13), channel_id=1, source_target_pairs={{0,1},{1,0},{2,3},{3,2},{4,5},{5,4},{6,7},{7,6},{8,9},{9,8},{10,11... | collective-permute-start | bytes 6920 | tf_op jit(solution)/shard_map/ppermute | solution.py:157
  11.6 0.0 copy-done.1
  11.6 0.8 %collective-permute-done.3 = f32[1,576]{1,0:T(1,128)S(1)} collective-permute-done((f32[1,576]{1,0:T(1,128)S(1)}, f32[1,576]{1,0:T(1,128)S(1)}, u32[]{:S(2)}, u32[]{:S(2)}) %collective-permute-start.3) | collective-permute-done | bytes 2336 | tf_op jit(solution)/shard_map/ppermute | solution.py:157
  12.4 0.1 broadcast_select_fusion.8
  12.5 1.7 %collective-permute-start.4 = (f32[1,1152]{1,0:T(1,128)S(1)}, f32[1,1152]{1,0:T(1,128)S(1)}, u32[]{:S(2)}, u32[]{:S(2)}) collective-permute-start(f32[1,1152]{1,0:T(1,128)S(1)} %broadcast_select_fusion.8), channel_id=1, source_target_pairs={{0,2},{1,3},{2,0},{3,1},{4,6},{5,7},{6,4},{7,5},{8,10},{9,11},{10,... | collective-permute-start | bytes 13832 | tf_op jit(solution)/shard_map/ppermute | solution.py:157
  14.2 0.1 maximum_select_fusion.1
  14.3 1.2 %collective-permute-done.4 = f32[1,1152]{1,0:T(1,128)S(1)} collective-permute-done((f32[1,1152]{1,0:T(1,128)S(1)}, f32[1,1152]{1,0:T(1,128)S(1)}, u32[]{:S(2)}, u32[]{:S(2)}) %collective-permute-start.4) | collective-permute-done | bytes 4640 | tf_op jit(solution)/shard_map/ppermute | solution.py:157
  15.5 3.1 %collective-permute-start.5 = (f32[1,2304]{1,0:T(1,128)S(1)}, f32[1,2304]{1,0:T(1,128)S(1)}, u32[]{:S(2)}, u32[]{:S(2)}) collective-permute-start(f32[1,2304]{1,0:T(1,128)S(1)} %broadcast_select_fusion.7), channel_id=1, source_target_pairs={{0,4},{1,5},{2,6},{3,7},{4,0},{5,1},{6,2},{7,3},{8,12},{9,13},{10,... | collective-permute-start | bytes 27656 | tf_op jit(solution)/shard_map/ppermute | solution.py:157
  18.6 3.0 %all-to-all-done = bf16[16,16,1152]{2,1,0:T(8,128)(2,1)S(1)} async-done(((bf16[16,16,1152]{2,1,0:T(8,128)(2,1)}), bf16[16,16,1152]{2,1,0:T(8,128)(2,1)S(1)}, u32[]{:S(2)}, u32[]{:S(2)}) %all-to-all-start) | async-done | bytes 589856 | tf_op jit(solution)/shard_map/all_to_all | solution.py:253
  21.6 0.1 convert_reduce_fusion.near_ref
  21.6 7.0 %collective-permute-start.6 = (f32[16,1152]{1,0:T(8,128)S(1)}, f32[16,1152]{1,0:T(8,128)S(1)}, u32[]{:S(2)}, u32[]{:S(2)}) collective-permute-start(f32[16,1152]{1,0:T(8,128)S(1)} %convert_reduce_fusion.near_ref), channel_id=1, source_target_pairs={{0,128},{8,136},{16,144},{24,152},{32,160},{40,168},{48,176},{56,1... | collective-permute-start | bytes 221192 | tf_op jit(solution)/shard_map/ppermute | solution.py:265
  28.6 0.0 collective-permute-done.5
  28.7 0.0 copy-done.3
  28.7 0.0 copy-done.4
  28.7 3.7 %score.1 = (f32[256,128]{1,0:T(8,128)S(1)}, f32[256,128]{1,0:T(8,128)S(1)}) custom-call(s32[1,8]{1,0:T(1,128)S(1)} %copy-done.3, s32[1,8]{1,0:T(1,128)S(1)} %copy-done.4, bf16[256,4608]{1,0:T(8,128)(2,1)} %hidden_ref.3, f32[1,4608]{1,0:T(1,128)S(1)} %broadcast_select_fusion.6.v_ref), custom_call_target="tpu_custom_call" | custom-call | flops 4718592 | bytes 2359296 | tf_op jit(solution)/shard_map/score/pallas_call | solution.py:85
  32.3 0.0 collective-permute-done.6.far_ref
  32.4 1.0 %average.1 = (s16[16,16,1280]{2,1,0:T(8,128)(2,1)}, f32[1,128]{1,0:T(1,128)S(1)}) custom-call(f32[16,1152]{1,0:T(8,128)S(1)} %convert_reduce_fusion.near_ref, f32[16,1152]{1,0:T(8,128)S(1)} %collective-permute-done.6.far_ref, f32[16,1152]{1,0:T(8,128)S(1)} %dynamic_slice.3.global_ref), custom_call_target="tpu_custom_call" | custom-call | flops 184320 | bytes 737280 | tf_op jit(solution)/shard_map/average/pallas_call | solution.py:180
  33.4 3.6 %all-to-all-start.1 = ((s16[16,16,1280]{2,1,0:T(8,128)(2,1)}), s16[16,16,1280]{2,1,0:T(8,128)(2,1)S(1)}, u32[]{:S(2)}, u32[]{:S(2)}) async-start(s16[16,16,1280]{2,1,0:T(8,128)(2,1)} %get-tuple-element.72), calls=%async_computation.1 | async-start | bytes 1310720 | tf_op jit(solution)/shard_map/all_to_all | solution.py:271
  37.0 2.2 %weigh.1 = f32[1,4608]{1,0:T(1,128)S(1)} custom-call(bf16[256,4608]{1,0:T(8,128)(2,1)} %hidden_ref.3, f32[256,128]{1,0:T(8,128)S(1)} %get-tuple-element.66.alpha_ref, f32[1,128]{1,0:T(1,128)S(1)} %get-tuple-element.70.mark_ref), custom_call_target="tpu_custom_call" | custom-call | flops 2359296 | bytes 2359296 | tf_op jit(solution)/shard_map/weigh/pallas_call | solution.py:111
  39.2 0.0 copy-start
  39.2 12.1 %conditional.1 = (bf16[256,4608]{1,0:T(8,128)(2,1)}, f32[1,576]{1,0:T(1,128)S(1)}) conditional(s32[]{:T(128)} %convert_element_type.12, (bf16[256,4608]{1,0:T(8,128)(2,1)}, f32[1,4608]{1,0:T(1,128)S(1)}, f32[256,128]{1,0:T(8,128)S(1)}, f32[256,128]{1,0:T(8,128)S(1)}, f32[1,4608]{1,0:T(1,128)S(1)}) %tuple.23, (s32[]{:T(128)}, f32[1,4608]{1,0:T(1,128)S(1)}, ...), branch_computations={%region_1.2_spmd, %region_2.3_spmd} | conditional | flops 7089990 | bytes 4896205 | solution.py:290
  39.3 1.3 %collective-permute-start = (f32[1,2304]{1,0:T(1,128)S(1)}, f32[1,2304]{1,0:T(1,128)S(1)}, u32[]{:S(2)}, u32[]{:S(2)}) collective-permute-start(f32[1,2304]{1,0:T(1,128)S(1)} %broadcast_select_fusion.1), channel_id=1, source_target_pairs={{0,4},{1,5},{2,6},{3,7},{4,0},{5,1},{6,2},{7,3},{8,12},{9,13},{10,... | collective-permute-start | bytes 27656 | tf_op jit(solution)/shard_map/cond/branch_1_fun/ppermute | solution.py:157
  40.5 3.4 %token_grad.3 = bf16[256,4608]{1,0:T(8,128)(2,1)} custom-call(bf16[256,4608]{1,0:T(8,128)(2,1)} %get-tuple-element.29.hidden_ref, f32[1,4608]{1,0:T(1,128)S(1)} %get-tuple-element.30.v_ref, f32[256,128]{1,0:T(8,128)S(1)} %get-tuple-element.31.alpha_ref, f32[256,128]{1,0:T(8,128)S(1)} %get-tuple-element.32.beta_ref), custom_call_target="tpu_custom_call" | custom-call | flops 7077888 | bytes 4718592 | tf_op jit(solution)/shard_map/cond/branch_1_fun/token_grad/pallas_call | solution.py:143
  43.9 0.0 collective-permute-done
  44.0 0.8 %collective-permute-start.1 = (f32[1,1152]{1,0:T(1,128)S(1)}, f32[1,1152]{1,0:T(1,128)S(1)}, u32[]{:S(2)}, u32[]{:S(2)}) collective-permute-start(f32[1,1152]{1,0:T(1,128)S(1)} %broadcast_select_fusion.2), channel_id=1, source_target_pairs={{0,2},{1,3},{2,0},{3,1},{4,6},{5,7},{6,4},{7,5},{8,10},{9,11},{10,... | collective-permute-start | bytes 13832 | tf_op jit(solution)/shard_map/cond/branch_1_fun/ppermute | solution.py:157
  44.8 2.0 %collective-permute-done.1 = f32[1,1152]{1,0:T(1,128)S(1)} collective-permute-done((f32[1,1152]{1,0:T(1,128)S(1)}, f32[1,1152]{1,0:T(1,128)S(1)}, u32[]{:S(2)}, u32[]{:S(2)}) %collective-permute-start.1) | collective-permute-done | bytes 4640 | tf_op jit(solution)/shard_map/cond/branch_1_fun/ppermute | solution.py:157
  46.8 0.1 broadcast_select_fusion.4
  46.9 3.6 %collective-permute-start.2 = (f32[1,576]{1,0:T(1,128)S(1)}, f32[1,576]{1,0:T(1,128)S(1)}, u32[]{:S(2)}, u32[]{:S(2)}) collective-permute-start(f32[1,576]{1,0:T(1,128)S(1)} %broadcast_select_fusion.4), channel_id=1, source_target_pairs={{0,1},{1,0},{2,3},{3,2},{4,5},{5,4},{6,7},{7,6},{8,9},{9,8},{10,11... | collective-permute-start | bytes 6920 | tf_op jit(solution)/shard_map/cond/branch_1_fun/ppermute | solution.py:157
  50.5 0.8 %collective-permute-done.2 = f32[1,576]{1,0:T(1,128)S(1)} collective-permute-done((f32[1,576]{1,0:T(1,128)S(1)}, f32[1,576]{1,0:T(1,128)S(1)}, u32[]{:S(2)}, u32[]{:S(2)}) %collective-permute-start.2) | collective-permute-done | bytes 2336 | tf_op jit(solution)/shard_map/cond/branch_1_fun/ppermute | solution.py:157
  51.3 0.1 fusion.2
  51.4 0.0 all-to-all-done.1.coded_ref
  51.4 0.0 copy-done
  51.4 0.0 copy-start.2
  51.4 1.3 %copy-done.2 = f32[64,4608]{1,0:T(8,128)S(1)} copy-done((f32[64,4608]{1,0:T(8,128)S(1)}, f32[64,4608]{1,0:T(8,128)}, u32[]{:S(2)}) %copy-start.2) | copy-done | bytes 1179672
  52.7 2.4 %update.1 = (f32[1,576]{1,0:T(1,128)}, f32[1,576]{1,0:T(1,128)}, f32[64,4608]{1,0:T(8,128)}, f32[64,4608]{1,0:T(8,128)}, bf16[64,4608]{1,0:T(8,128)(2,1)}) custom-call(s16[16,16,1280]{2,1,0:T(8,128)(2,1)S(1)} %all-to-all-done.1.coded_ref, f32[1,576]{1,0:T(1,128)S(1)} %get-tuple-element.73.w_ref, f32[1,576]{1,0:T(1,128)S(1)} %broadcast_in_dim.9.gain_ref, ...), custom_call_target="tpu_custom_call" | custom-call | flops 2949120 | bytes 6488064 | tf_op jit(solution)/shard_map/update/pallas_call | solution.py:230
  (16 shorter events, 0.2 us)
Async XLA Ops:
  1.8 8.6 %copy-start.5 = (bf16[576]{0:T(1024)(128)(2,1)S(1)}, bf16[576]{0:T(1024)(128)(2,1)}, u32[]{:S(2)}) copy-start(bf16[576]{0:T(1024)(128)(2,1)} %param.13) | copy-start | bytes 3460
  1.9 8.6 %copy-start.6 = (bf16[576]{0:T(1024)(128)(2,1)S(1)}, bf16[576]{0:T(1024)(128)(2,1)}, u32[]{:S(2)}) copy-start(bf16[576]{0:T(1024)(128)(2,1)} %param.14) | copy-start | bytes 3460
  1.9 9.7 %copy-start.1 = (f32[64,4608]{1,0:T(8,128)S(1)}, f32[64,4608]{1,0:T(8,128)}, u32[]{:S(2)}) copy-start(f32[64,4608]{1,0:T(8,128)} %global_ref.1) | copy-start | bytes 3538948
  2.8 25.9 %copy-start.3 = (s32[1,8]{1,0:T(1,128)S(1)}, s32[1,8]{1,0:T(1,128)}, u32[]{:S(2)}) copy-start(s32[1,8]{1,0:T(1,128)} %lengths_ref.1) | copy-start | bytes 100
  2.8 25.9 %copy-start.4 = (s32[1,8]{1,0:T(1,128)S(1)}, s32[1,8]{1,0:T(1,128)}, u32[]{:S(2)}) copy-start(s32[1,8]{1,0:T(1,128)} %ranks_ref.1) | copy-start | bytes 100
  2.8 18.8 %all-to-all-start = ((bf16[16,16,1152]{2,1,0:T(8,128)(2,1)}), bf16[16,16,1152]{2,1,0:T(8,128)(2,1)S(1)}, u32[]{:S(2)}, u32[]{:S(2)}) async-start(bf16[16,16,1152]{2,1,0:T(8,128)(2,1)} %bitcast.1), calls=%async_computation | async-start | bytes 1179648 | tf_op jit(solution)/shard_map/all_to_all | solution.py:253
  10.5 1.9 %collective-permute-start.3 = (f32[1,576]{1,0:T(1,128)S(1)}, f32[1,576]{1,0:T(1,128)S(1)}, u32[]{:S(2)}, u32[]{:S(2)}) collective-permute-start(f32[1,576]{1,0:T(1,128)S(1)} %mul.13), channel_id=1, source_target_pairs={{0,1},{1,0},{2,3},{3,2},{4,5},{5,4},{6,7},{7,6},{8,9},{9,8},{10,11... | collective-permute-start | bytes 6920 | tf_op jit(solution)/shard_map/ppermute | solution.py:157
  12.5 3.0 %collective-permute-start.4 = (f32[1,1152]{1,0:T(1,128)S(1)}, f32[1,1152]{1,0:T(1,128)S(1)}, u32[]{:S(2)}, u32[]{:S(2)}) collective-permute-start(f32[1,1152]{1,0:T(1,128)S(1)} %broadcast_select_fusion.8), channel_id=1, source_target_pairs={{0,2},{1,3},{2,0},{3,1},{4,6},{5,7},{6,4},{7,5},{8,10},{9,11},{10,... | collective-permute-start | bytes 13832 | tf_op jit(solution)/shard_map/ppermute | solution.py:157
  15.5 13.1 %collective-permute-start.5 = (f32[1,2304]{1,0:T(1,128)S(1)}, f32[1,2304]{1,0:T(1,128)S(1)}, u32[]{:S(2)}, u32[]{:S(2)}) collective-permute-start(f32[1,2304]{1,0:T(1,128)S(1)} %broadcast_select_fusion.7), channel_id=1, source_target_pairs={{0,4},{1,5},{2,6},{3,7},{4,0},{5,1},{6,2},{7,3},{8,12},{9,13},{10,... | collective-permute-start | bytes 27656 | tf_op jit(solution)/shard_map/ppermute | solution.py:157
  21.6 10.7 %collective-permute-start.6 = (f32[16,1152]{1,0:T(8,128)S(1)}, f32[16,1152]{1,0:T(8,128)S(1)}, u32[]{:S(2)}, u32[]{:S(2)}) collective-permute-start(f32[16,1152]{1,0:T(8,128)S(1)} %convert_reduce_fusion.near_ref), channel_id=1, source_target_pairs={{0,128},{8,136},{16,144},{24,152},{32,160},{40,168},{48,176},{56,1... | collective-permute-start | bytes 221192 | tf_op jit(solution)/shard_map/ppermute | solution.py:265
  33.4 18.0 %all-to-all-start.1 = ((s16[16,16,1280]{2,1,0:T(8,128)(2,1)}), s16[16,16,1280]{2,1,0:T(8,128)(2,1)S(1)}, u32[]{:S(2)}, u32[]{:S(2)}) async-start(s16[16,16,1280]{2,1,0:T(8,128)(2,1)} %get-tuple-element.72), calls=%async_computation.1 | async-start | bytes 1310720 | tf_op jit(solution)/shard_map/all_to_all | solution.py:271
  39.2 12.2 %copy-start = (bf16[1,64,4608]{2,1,0:T(8,128)(2,1)S(1)}, bf16[1,64,4608]{2,1,0:T(8,128)(2,1)}, u32[]{:S(2)}) copy-start(bf16[1,64,4608]{2,1,0:T(8,128)(2,1)} %param.15) | copy-start | bytes 1769476
  39.3 4.7 %collective-permute-start = (f32[1,2304]{1,0:T(1,128)S(1)}, f32[1,2304]{1,0:T(1,128)S(1)}, u32[]{:S(2)}, u32[]{:S(2)}) collective-permute-start(f32[1,2304]{1,0:T(1,128)S(1)} %broadcast_select_fusion.1), channel_id=1, source_target_pairs={{0,4},{1,5},{2,6},{3,7},{4,0},{5,1},{6,2},{7,3},{8,12},{9,13},{10,... | collective-permute-start | bytes 27656 | tf_op jit(solution)/shard_map/cond/branch_1_fun/ppermute | solution.py:157
  44.0 2.8 %collective-permute-start.1 = (f32[1,1152]{1,0:T(1,128)S(1)}, f32[1,1152]{1,0:T(1,128)S(1)}, u32[]{:S(2)}, u32[]{:S(2)}) collective-permute-start(f32[1,1152]{1,0:T(1,128)S(1)} %broadcast_select_fusion.2), channel_id=1, source_target_pairs={{0,2},{1,3},{2,0},{3,1},{4,6},{5,7},{6,4},{7,5},{8,10},{9,11},{10,... | collective-permute-start | bytes 13832 | tf_op jit(solution)/shard_map/cond/branch_1_fun/ppermute | solution.py:157
  46.9 4.4 %collective-permute-start.2 = (f32[1,576]{1,0:T(1,128)S(1)}, f32[1,576]{1,0:T(1,128)S(1)}, u32[]{:S(2)}, u32[]{:S(2)}) collective-permute-start(f32[1,576]{1,0:T(1,128)S(1)} %broadcast_select_fusion.4), channel_id=1, source_target_pairs={{0,1},{1,0},{2,3},{3,2},{4,5},{5,4},{6,7},{7,6},{8,9},{9,8},{10,11... | collective-permute-start | bytes 6920 | tf_op jit(solution)/shard_map/cond/branch_1_fun/ppermute | solution.py:157
  51.4 1.3 %copy-start.2 = (f32[64,4608]{1,0:T(8,128)S(1)}, f32[64,4608]{1,0:T(8,128)}, u32[]{:S(2)}) copy-start(f32[64,4608]{1,0:T(8,128)} %momentum_ref.1) | copy-start | bytes 3538948

commit v4 on v3

--- a/solution.py
+++ b/solution.py
@@ -20,14 +20,25 @@
 
 PLANES = 2
 PLANE = 16
-TALL, BROAD = 16, 1152
+TALL, BROAD = 8, 2304
 LARGEST = 10.0
 STEPS = 32767.0
 SHARES = 4
+WHOLE_VMEM = 60 * 1024 * 1024
+BANDS = 4
 VMEM_LIMIT = 16 * 1024 * 1024
-
-
-def score_kernel(lengths_ref, ranks_ref, hidden_ref, v_ref, alpha_ref, beta_ref, square_ref, dot_ref):
+SCORE_LIMIT = 16 * 1024 * 1024
+TOKEN_LIMIT = 16 * 1024 * 1024
+CHUNKS = 4
+
+
+def chunk_copies(source, kept, sem):
+    rows = kept.shape[0] // CHUNKS
+    parts = [pl.ds(n * rows, rows) for n in range(CHUNKS)]
+    return [pltpu.make_async_copy(source.at[parts[n]], kept.at[parts[n]], sem.at[n]) for n in range(CHUNKS)]
+
+
+def score_kernel(lengths_ref, ranks_ref, hidden_ref, v_ref, alpha_ref, beta_ref, w_ref, square_ref, dot_ref):
     tokens, width = hidden_ref.shape
 
     def first(step, carry):
@@ -76,26 +87,6 @@
     alpha_ref[...] = jnp.broadcast_to(alpha, alpha_ref.shape)
     beta_ref[...] = jnp.broadcast_to(alpha * inverse * inverse * dots / width, beta_ref.shape)
 
-
-def score_call(lengths, ranks, hidden, v):
-    tokens, width = hidden.shape
-    smem = pl.BlockSpec(memory_space=pltpu.SMEM)
-    vmem = pl.BlockSpec(memory_space=pltpu.VMEM)
-    wide = jax.ShapeDtypeStruct((tokens, LANES), jnp.float32)
-    return pl.pallas_call(
-        score_kernel,
-        out_shape=(wide, wide),
-        in_specs=[smem, smem, vmem, vmem],
-        out_specs=(vmem, vmem),
-        scratch_shapes=[pltpu.VMEM((tokens, 1), jnp.float32)] * 2,
-        compiler_params=pltpu.CompilerParams(vmem_limit_bytes=VMEM_LIMIT),
-        cost_estimate=pl.CostEstimate(flops=4 * tokens * width, bytes_accessed=2 * tokens * width, transcendentals=0),
-        name="score",
-    )(lengths, ranks, hidden, v)
-
-
-def weigh_kernel(hidden_ref, alpha_ref, mark_ref, w_ref):
-    tokens, width = hidden_ref.shape
     for j in range(width // LANES):
         part = slice(j * LANES, (j + 1) * LANES)
         total = jnp.zeros((ROWS, LANES), jnp.float32)
@@ -105,48 +96,57 @@
         w_ref[:, part] = jnp.sum(total, axis=0, keepdims=True) * (1.0 / LOSS_SCALE)
 
 
-def weigh_call(hidden, alpha, mark):
+def score_call(lengths, ranks, hidden, v):
     tokens, width = hidden.shape
+    smem = pl.BlockSpec(memory_space=pltpu.SMEM)
     vmem = pl.BlockSpec(memory_space=pltpu.VMEM)
-    return pl.pallas_call(
-        weigh_kernel,
-        out_shape=jax.ShapeDtypeStruct((1, width), jnp.float32),
-        in_specs=[vmem] * 3,
-        out_specs=vmem,
-        compiler_params=pltpu.CompilerParams(vmem_limit_bytes=VMEM_LIMIT),
-        cost_estimate=pl.CostEstimate(flops=2 * tokens * width, bytes_accessed=2 * tokens * width, transcendentals=0),
-        name="weigh",
-    )(hidden, alpha, mark)
-
-
-def token_kernel(hidden_ref, v_ref, alpha_ref, beta_ref, out_ref, kept_ref, sem):
-    tokens, width = hidden_ref.shape
-    copies = []
-    for band in range(width // BROAD):
-        for j in range(BROAD // LANES):
-            part = slice(band * BROAD + j * LANES, band * BROAD + (j + 1) * LANES)
+    wide = jax.ShapeDtypeStruct((tokens, LANES), jnp.float32)
+    return pl.pallas_call(
+        score_kernel,
+        out_shape=(wide, wide, jax.ShapeDtypeStruct((1, width), jnp.float32)),
+        in_specs=[smem, smem, vmem, vmem],
+        out_specs=(vmem, vmem, vmem),
+        scratch_shapes=[pltpu.VMEM((tokens, 1), jnp.float32)] * 2,
+        compiler_params=pltpu.CompilerParams(vmem_limit_bytes=SCORE_LIMIT),
+        cost_estimate=pl.CostEstimate(flops=6 * tokens * width, bytes_accessed=2 * tokens * width, transcendentals=0),
+        name="score",
+    )(lengths, ranks, hidden, v)
+
+
+def token_kernel(hidden_hbm_ref, v_ref, alpha_ref, beta_ref, out_ref, hidden_ref, kept_ref, in_sem, out_sem):
+    tokens, width = hidden_hbm_ref.shape
+    arrivals = chunk_copies(hidden_hbm_ref, hidden_ref, in_sem)
+    for arrival in arrivals:
+        arrival.start()
+    departures = []
+    rows_each = tokens // CHUNKS
+    for n, arrival in enumerate(arrivals):
+        arrival.wait()
+        for j in range(width // LANES):
+            part = slice(j * LANES, (j + 1) * LANES)
             v = v_ref[:, part]
-            for row in range(0, tokens, ROWS):
+            for row in range(n * rows_each, (n + 1) * rows_each, ROWS):
                 rows = slice(row, row + ROWS)
                 values = hidden_ref[rows, part].astype(jnp.float32)
                 kept_ref[rows, part] = (alpha_ref[rows, :] * v - beta_ref[rows, :] * values).astype(kept_ref.dtype)
-        columns = slice(band * BROAD, (band + 1) * BROAD)
-        copies.append(pltpu.make_async_copy(kept_ref.at[:, columns], out_ref.at[:, columns], sem.at[band]))
-        copies[-1].start()
-    for copy in copies:
-        copy.wait()
+        here = pl.ds(n * rows_each, rows_each)
+        departures.append(pltpu.make_async_copy(kept_ref.at[here], out_ref.at[here], out_sem.at[n]))
+        departures[-1].start()
+    for departure in departures:
+        departure.wait()
 
 
 def token_call(hidden, v, alpha, beta):
     tokens, width = hidden.shape
     vmem = pl.BlockSpec(memory_space=pltpu.VMEM)
+    whole = pl.BlockSpec(memory_space=pl.ANY)
     return pl.pallas_call(
         token_kernel,
         out_shape=jax.ShapeDtypeStruct((tokens, width), jnp.bfloat16),
-        in_specs=[vmem] * 4,
-        out_specs=pl.BlockSpec(memory_space=pl.ANY),
-        scratch_shapes=[pltpu.VMEM((tokens, width), jnp.bfloat16), pltpu.SemaphoreType.DMA((width // BROAD,))],
-        compiler_params=pltpu.CompilerParams(vmem_limit_bytes=VMEM_LIMIT),
+        in_specs=[whole] + [vmem] * 3,
+        out_specs=whole,
+        scratch_shapes=[pltpu.VMEM((tokens, width), jnp.bfloat16)] * 2 + [pltpu.SemaphoreType.DMA((CHUNKS,))] * 2,
+        compiler_params=pltpu.CompilerParams(vmem_limit_bytes=TOKEN_LIMIT),
         cost_estimate=pl.CostEstimate(flops=6 * tokens * width, bytes_accessed=4 * tokens * width, transcendentals=0),
         name="token_grad",
     )(hidden, v, alpha, beta)
@@ -157,7 +157,28 @@
     return lax.ppermute(array, "fsdp", [(i, i ^ k) for i in range(devices)])
 
 
-def average_kernel(near_ref, far_ref, global_ref, out_ref, mark_ref, coded_ref, sem):
+def own_kernel(at_ref, global_ref, out_ref, sem):
+    rows = pl.ds(pl.multiple_of(at_ref[0, 0] * TALL, TALL), TALL)
+    columns = pl.ds(pl.multiple_of(at_ref[0, 1] * BROAD, BROAD), BROAD)
+    copy = pltpu.make_async_copy(global_ref.at[rows, columns], out_ref, sem)
+    copy.start()
+    copy.wait()
+
+
+def own_call(at, global_prev):
+    return pl.pallas_call(
+        own_kernel,
+        out_shape=jax.ShapeDtypeStruct((TALL, BROAD), global_prev.dtype),
+        in_specs=[pl.BlockSpec(memory_space=pltpu.SMEM), pl.BlockSpec(memory_space=pl.ANY)],
+        out_specs=pl.BlockSpec(memory_space=pltpu.VMEM),
+        scratch_shapes=[pltpu.SemaphoreType.DMA],
+        compiler_params=pltpu.CompilerParams(vmem_limit_bytes=WHOLE_VMEM),
+        cost_estimate=pl.CostEstimate(flops=0, bytes_accessed=8 * TALL * BROAD, transcendentals=0),
+        name="own",
+    )(at, global_prev)
+
+
+def average_kernel(near_ref, far_ref, global_ref, out_ref, coded_ref, sem):
     average = global_ref[...] - (near_ref[...] + far_ref[...]) * (1.0 / (PLANES * PLANE))
     top = jnp.max(jnp.abs(average), axis=1, keepdims=True)
     unit = jnp.clip(jnp.ceil(top * (STEPS / LARGEST)), 1.0, STEPS)
@@ -168,7 +189,6 @@
         coded_ref[part, :, BROAD:] = jnp.broadcast_to(unit, (TALL, LANES)).astype(jnp.int32).astype(coded_ref.dtype)
     for part in range(PLANE // SHARES):
         copies.append(pltpu.make_async_copy(coded_ref, out_ref.at[pl.ds(part * SHARES, SHARES)], sem.at[part]))
-    mark_ref[...] = jnp.zeros_like(mark_ref)
     for copy in copies:
         copy.start()
     for copy in copies:
@@ -179,9 +199,9 @@
     vmem = pl.BlockSpec(memory_space=pltpu.VMEM)
     return pl.pallas_call(
         average_kernel,
-        out_shape=(jax.ShapeDtypeStruct((PLANE, TALL, BROAD + LANES), jnp.int16), jax.ShapeDtypeStruct((1, LANES), jnp.float32)),
+        out_shape=jax.ShapeDtypeStruct((PLANE, TALL, BROAD + LANES), jnp.int16),
         in_specs=[vmem, vmem, vmem],
-        out_specs=(pl.BlockSpec(memory_space=pl.ANY), vmem),
+        out_specs=pl.BlockSpec(memory_space=pl.ANY),
         scratch_shapes=[pltpu.VMEM((SHARES, TALL, BROAD + LANES), jnp.int16), pltpu.SemaphoreType.DMA((PLANE // SHARES,))],
         compiler_params=pltpu.CompilerParams(vmem_limit_bytes=VMEM_LIMIT),
         cost_estimate=pl.CostEstimate(flops=10 * near.size, bytes_accessed=40 * near.size, transcendentals=0),
@@ -196,21 +216,25 @@
     across = width // BROAD
     new_global_ref, new_momentum_ref, merged_ref = kept
     copies = []
-    for band in range(rows // TALL):
-        row = slice(band * TALL, (band + 1) * TALL)
-        for column in range(across):
-            p = band * across + column
+    band_rows, band_pieces = rows // BANDS, PLANE // BANDS
+    for band in range(BANDS):
+        for p in range(band * band_pieces, (band + 1) * band_pieces):
+            row = slice(p // across * TALL, (p // across + 1) * TALL)
             scale = coded_ref[p, :, BROAD:].astype(jnp.int32).astype(jnp.float32) * (LARGEST / (STEPS * STEPS))
             for j in range(BROAD // LANES):
-                part = slice(column * BROAD + j * LANES, column * BROAD + (j + 1) * LANES)
+                at = p % across * BROAD + j * LANES
+                part = slice(at, at + LANES)
                 steps = coded_ref[p, :, j * LANES:(j + 1) * LANES].astype(jnp.int32).astype(jnp.float32)
                 average = steps * scale
                 new_momentum = MOMENTUM * momentum_ref[row, part] + average
                 new_global = global_ref[row, part] - OUTER_RATE * (MOMENTUM * new_momentum + average)
                 new_momentum_ref[row, part] = new_momentum
                 new_global_ref[row, part] = new_global
-                merged = MIXING * local_ref[row, part].astype(jnp.float32) + (1.0 - MIXING) * new_global
-                merged_ref[row, part] = merged.astype(merged_ref.dtype)
+        row = slice(band * band_rows, (band + 1) * band_rows)
+        for j in range(width // LANES):
+            part = slice(j * LANES, (j + 1) * LANES)
+            merged = MIXING * local_ref[row, part].astype(jnp.float32) + (1.0 - MIXING) * new_global_ref[row, part]
+            merged_ref[row, part] = merged.astype(merged_ref.dtype)
         for n in range(3):
             copies.append(pltpu.make_async_copy(kept[n].at[row, :], outs[n].at[row, :], sem.at[n, band]))
             copies[-1].start()
@@ -233,7 +257,7 @@
         in_specs=[vmem] * 7,
         out_specs=(vmem,) * 2 + (whole,) * 3,
         scratch_shapes=[pltpu.VMEM((rows, width), t) for t in (wide, wide, narrow)]
-        + [pltpu.SemaphoreType.DMA((3, rows // TALL))],
+        + [pltpu.SemaphoreType.DMA((3, BANDS))],
         compiler_params=pltpu.CompilerParams(vmem_limit_bytes=VMEM_LIMIT),
         cost_estimate=pl.CostEstimate(flops=10 * rows * width, bytes_accessed=22 * rows * width, transcendentals=0),
         name="update",
@@ -247,7 +271,7 @@
     here = lax.axis_index("fsdp")
     local = local_frag[0]
 
-    pieces = local.reshape(4, TALL, 4, BROAD).transpose(0, 2, 1, 3).reshape(PLANE, TALL, BROAD)
+    pieces = local.reshape(8, TALL, 2, BROAD).transpose(0, 2, 1, 3).reshape(PLANE, TALL, BROAD)
     pieces, gain, head = barrier((pieces, gain, head))
     gain_wide, head_wide = gain.astype(jnp.float32)[None], head.astype(jnp.float32)[None]
     mine = lax.all_to_all(pieces, "rep", 0, 0, tiled=True, axis_index_groups=planes)
@@ -258,16 +282,17 @@
         v = jnp.where(here & bit == 0, jnp.concatenate([v, other], 1), jnp.concatenate([other, v], 1))
     owned = lax.rem(lax.axis_index("rep"), PLANE)
     across = global_prev.shape[1] // BROAD
-    own_global = lax.dynamic_slice(global_prev, (owned // across * TALL, owned % across * BROAD), (TALL, BROAD))
+    own_global = own_call(jnp.stack([owned // across, owned % across]).astype(jnp.int32)[None], global_prev)
 
     mine, own_global = barrier((mine, own_global))
     near = jnp.sum(mine.astype(jnp.float32), axis=0)
     far = lax.ppermute(near, "rep", [(i, (i + PLANE) % replicas) for i in range(replicas)])
 
-    alpha, beta = score_call(lengths, ranks, hidden, v)
-    far, alpha, beta = barrier((far, alpha, beta))
-
-    coded, mark = average_call(near, far, own_global)
+    alpha, beta, w = score_call(lengths, ranks, hidden, v)
+    far, alpha, beta, w = barrier((far, alpha, beta, w))
+
+    coded = average_call(near, far, own_global)
+    coded, w = barrier((coded, w))
     received = lax.all_to_all(coded, "rep", 0, 0, tiled=True, axis_index_groups=planes)
 
     def halve(hidden, v, alpha, beta, w):
@@ -286,7 +311,6 @@
     def no_halving(hidden, v, alpha, beta, w):
         return token_call(hidden, v, alpha, beta), w[:, :w.shape[1] // devices]
 
-    w = weigh_call(hidden, alpha, mark)
     d_hidden, w = lax.cond(
         lax.axis_index("rep") < replicas, halve, no_halving, hidden, v, alpha, beta, w
     )

time: 55.5 us -> 50.6 us (0.912)
  waiting for transfers between devices: 7.81 us -> 4.87 us
  local copies, waits for them, and re-layouts: 3.42 us -> 1.34 us
  Pallas kernels: 12.6 us -> 11.3 us
  starting transfers between devices: 29.8 us -> 30.6 us
  other arithmetic: 0.51 us -> 1.1 us
    all_to_all x1, waiting for transfers between devices: 2.96 us -> 0.96 us  [body(): lax.all_to_all(pieces, 'rep', 0, 0, tiled=True, axis_index_groups=planes)]
    another operation x1 -> x0, local copies, waits for them, and re-layouts: 1.21 us -> none  [body(): local.reshape(4, TALL, 4, BROAD).transpose(0, 2, 1, 3)]
    ppermute x6, waiting for transfers between devices: 4.85 us -> 3.91 us  [along(): return lax.ppermute(array, 'fsdp', [(i, i ^ k) for i in range(devices)])]
    transpose x1 -> x0, local copies, waits for them, and re-layouts: 0.88 us -> none  [body(): local.reshape(4, TALL, 4, BROAD).transpose(0, 2, 1, 3)]
    pallas_call x3, Pallas kernels: 6.84 us -> 6.19 us  [the longest x1 3.02 us: score_call(): pl.pallas_call(score_kernel, out_shape=(wide, wide, jax.ShapeDtypeStruct(...]
    pallas_call x1, Pallas kernels: 3.36 us -> 2.75 us  [token_call(): pl.pallas_call(token_kernel, out_shape=jax.ShapeDtypeStruct((tokens, widt...]
    broadcast_in_dim x0 -> x1, other arithmetic: none -> 0.58 us  [body(): jnp.stack([owned // across, owned % across]).astype(jnp.int32)[None]]
    unnamed x14 -> x18, local copies, waits for them, and re-layouts: 1.3 us -> 1.31 us
  transfers between devices with their start and end apart: 9 -> 9, of which waited for: 5 -> 4; matrix products, arithmetic and copies ran while one was open for 1% -> 2% of each run, Pallas kernels for 17% -> 16%
where the time goes in v4:
time: 50.6 us; the launch traced here: 50.1 us
  starting transfers between devices  30.6 us (60%)
  Pallas kernels  11.3 us (22%)
  waiting for transfers between devices  4.87 us (10%)
  local copies, waits for them, and re-layouts  1.34 us (3%)
  other arithmetic  1.1 us (2%)
  between operations  0.89 us (2%)
    ppermute x6, starting transfers between devices, along(): return lax.ppermute(array, 'fsdp', [(i, i ^ k) for i in range(devices)])  11.8 us
    all_to_all x1, starting transfers between devices, body(): lax.all_to_all(pieces, 'rep', 0, 0, tiled=True, axis_index_groups=planes)  7.73 us
    ppermute x1, starting transfers between devices, body(): lax.ppermute(near, 'rep', [(i, (i + PLANE) % replicas) for i in range(rep...  7 us
    all_to_all x1, starting transfers between devices, body(): lax.all_to_all(coded, 'rep', 0, 0, tiled=True, axis_index_groups=planes)  4.02 us
    ppermute x6, waiting for transfers between devices, along(): return lax.ppermute(array, 'fsdp', [(i, i ^ k) for i in range(devices)])  3.91 us
    pallas_call x1, Pallas kernels, score_call(): pl.pallas_call(score_kernel, out_shape=(wide, wide, jax.ShapeDtypeStruct(...  3.02 us
    pallas_call x1, Pallas kernels, token_call(): pl.pallas_call(token_kernel, out_shape=jax.ShapeDtypeStruct((tokens, widt...  2.75 us
    pallas_call x1, Pallas kernels, update_call(): pl.pallas_call(update_kernel, out_shape=(grad, grad) + tuple((jax.ShapeDt...  2.37 us
  transfers between devices with their start and end apart: 9, of which 4 were waited for; matrix products, arithmetic and copies ran while one was open for 2% of the time, Pallas kernels for 16%

profile of v4, /device:TPU:1, one launch (start us, length us, event | category | flops | bytes accessed | tf_op | source)
XLA Modules:
  0.0 50.1 jit_solution(14520968460479595279)
XLA Ops:
  0.6 0.0 copy-start.8
  0.6 0.0 copy-start.7
  0.7 0.0 copy-start.6
  0.7 7.7 %all-to-all-start = ((bf16[16,8,2304]{2,1,0:T(8,128)(2,1)}), bf16[16,8,2304]{2,1,0:T(8,128)(2,1)S(1)}, u32[]{:S(2)}, u32[]{:S(2)}) async-start(bf16[16,8,2304]{2,1,0:T(8,128)(2,1)} %bitcast.11), calls=%async_computation | async-start | bytes 1179648 | tf_op jit(solution)/shard_map/all_to_all | solution.py:277
  8.4 0.0 copy-done.8
  8.4 0.0 copy-done.7
  8.4 0.0 copy-start.4
  8.4 0.0 copy-start.5
  8.5 1.0 %collective-permute-start.3 = (f32[1,576]{1,0:T(1,128)S(1)}, f32[1,576]{1,0:T(1,128)S(1)}, u32[]{:S(2)}, u32[]{:S(2)}) collective-permute-start(f32[1,576]{1,0:T(1,128)S(1)} %mul.7), channel_id=1, source_target_pairs={{0,1},{1,0},{2,3},{3,2},{4,5},{5,4},{6,7},{7,6},{8,9},{9,8},{10,11... | collective-permute-start | bytes 6920 | tf_op jit(solution)/shard_map/ppermute | solution.py:157
  9.5 0.6 %add_bitcast_fusion.at_ref = s32[1,2]{1,0:T(1,128)} fusion(s32[1]{0:T(128)} %bitcast.4, s32[1]{0:T(128)} %bitcast.3), kind=kLoop, calls=%fused_computation.16 | loop fusion | flops 2 | bytes 16 | tf_op jit(solution)/shard_map/broadcast_in_dim | solution.py:285
  10.1 2.2 %own.1.global_ref = f32[8,2304]{1,0:T(8,128)} custom-call(s32[1,2]{1,0:T(1,128)} %add_bitcast_fusion.at_ref, f32[64,4608]{1,0:T(8,128)} %global_ref.3), custom_call_target="tpu_custom_call" | custom-call | bytes 147456 | tf_op jit(solution)/shard_map/own/pallas_call | solution.py:169
  12.3 0.0 collective-permute-done.3
  12.3 0.1 broadcast_select_fusion.8
  12.4 1.7 %collective-permute-start.4 = (f32[1,1152]{1,0:T(1,128)S(1)}, f32[1,1152]{1,0:T(1,128)S(1)}, u32[]{:S(2)}, u32[]{:S(2)}) collective-permute-start(f32[1,1152]{1,0:T(1,128)S(1)} %broadcast_select_fusion.8), channel_id=1, source_target_pairs={{0,2},{1,3},{2,0},{3,1},{4,6},{5,7},{6,4},{7,5},{8,10},{9,11},{10,... | collective-permute-start | bytes 13832 | tf_op jit(solution)/shard_map/ppermute | solution.py:157
  14.1 0.1 maximum_select_fusion.1
  14.2 1.2 %collective-permute-done.4 = f32[1,1152]{1,0:T(1,128)S(1)} collective-permute-done((f32[1,1152]{1,0:T(1,128)S(1)}, f32[1,1152]{1,0:T(1,128)S(1)}, u32[]{:S(2)}, u32[]{:S(2)}) %collective-permute-start.4) | collective-permute-done | bytes 4640 | tf_op jit(solution)/shard_map/ppermute | solution.py:157
  15.4 3.1 %collective-permute-start.5 = (f32[1,2304]{1,0:T(1,128)S(1)}, f32[1,2304]{1,0:T(1,128)S(1)}, u32[]{:S(2)}, u32[]{:S(2)}) collective-permute-start(f32[1,2304]{1,0:T(1,128)S(1)} %broadcast_select_fusion.7), channel_id=1, source_target_pairs={{0,4},{1,5},{2,6},{3,7},{4,0},{5,1},{6,2},{7,3},{8,12},{9,13},{10,... | collective-permute-start | bytes 27656 | tf_op jit(solution)/shard_map/ppermute | solution.py:157
  18.5 1.0 %all-to-all-done = bf16[16,8,2304]{2,1,0:T(8,128)(2,1)S(1)} async-done(((bf16[16,8,2304]{2,1,0:T(8,128)(2,1)}), bf16[16,8,2304]{2,1,0:T(8,128)(2,1)S(1)}, u32[]{:S(2)}, u32[]{:S(2)}) %all-to-all-start) | async-done | bytes 589856 | tf_op jit(solution)/shard_map/all_to_all | solution.py:277
  19.5 0.1 convert_reduce_fusion.near_ref
  19.6 7.0 %collective-permute-start.6 = (f32[8,2304]{1,0:T(8,128)S(1)}, f32[8,2304]{1,0:T(8,128)S(1)}, u32[]{:S(2)}, u32[]{:S(2)}) collective-permute-start(f32[8,2304]{1,0:T(8,128)S(1)} %convert_reduce_fusion.near_ref), channel_id=1, source_target_pairs={{0,128},{8,136},{16,144},{24,152},{32,160},{40,168},{48,176},{56,1... | collective-permute-start | bytes 221192 | tf_op jit(solution)/shard_map/ppermute | solution.py:289
  26.5 0.0 collective-permute-done.5
  26.6 0.0 copy-done.6
  26.6 0.0 copy-done.4
  26.6 0.0 copy-done.5
  26.6 0.0 copy-start.3
  26.6 3.0 %score.1 = (f32[256,128]{1,0:T(8,128)S(1)}, f32[256,128]{1,0:T(8,128)S(1)}, f32[1,4608]{1,0:T(1,128)S(1)}) custom-call(s32[1,8]{1,0:T(1,128)S(1)} %copy-done.4, s32[1,8]{1,0:T(1,128)S(1)} %copy-done.5, bf16[256,4608]{1,0:T(8,128)(2,1)S(1)} %copy-done.6, f32[1,4608]{1,0:T(1,128)S(1)} %broadcast_select_fusion.6.v_ref), custom_call_target="tpu_custom_call" | custom-call | flops 7077888 | bytes 2359296 | tf_op jit(solution)/shard_map/score/pallas_call | solution.py:104
  29.6 0.0 collective-permute-done.6.far_ref
  29.7 0.0 copy-done.3
  29.7 1.0 %average.1 = s16[16,8,2432]{2,1,0:T(8,128)(2,1)} custom-call(f32[8,2304]{1,0:T(8,128)S(1)} %convert_reduce_fusion.near_ref, f32[8,2304]{1,0:T(8,128)S(1)} %collective-permute-done.6.far_ref, f32[8,2304]{1,0:T(8,128)S(1)} %copy-done.3), custom_call_target="tpu_custom_call" | custom-call | flops 184320 | bytes 737280 | tf_op jit(solution)/shard_map/average/pallas_call | solution.py:200
  30.7 4.0 %all-to-all-start.1 = ((s16[16,8,2432]{2,1,0:T(8,128)(2,1)}), s16[16,8,2432]{2,1,0:T(8,128)(2,1)S(1)}, u32[]{:S(2)}, u32[]{:S(2)}) async-start(s16[16,8,2432]{2,1,0:T(8,128)(2,1)} %average.1), calls=%async_computation.1 | async-start | bytes 1245184 | tf_op jit(solution)/shard_map/all_to_all | solution.py:296
  34.7 0.0 copy-start
  34.7 0.0 copy-start.1
  34.7 11.8 %conditional.1 = (bf16[256,4608]{1,0:T(8,128)(2,1)}, f32[1,576]{1,0:T(1,128)S(1)}) conditional(s32[]{:T(128)} %convert_element_type.12, (bf16[256,4608]{1,0:T(8,128)(2,1)}, f32[1,4608]{1,0:T(1,128)S(1)}, f32[256,128]{1,0:T(8,128)S(1)}, f32[256,128]{1,0:T(8,128)S(1)}, f32[1,4608]{1,0:T(1,128)S(1)}) %tuple.25, (s32[]{:T(128)}, f32[1,4608]{1,0:T(1,128)S(1)}, ...), branch_computations={%region_1.2_spmd, %region_2.3_spmd} | conditional | flops 7089990 | bytes 4896205 | solution.py:314
  34.8 1.3 %collective-permute-start = (f32[1,2304]{1,0:T(1,128)S(1)}, f32[1,2304]{1,0:T(1,128)S(1)}, u32[]{:S(2)}, u32[]{:S(2)}) collective-permute-start(f32[1,2304]{1,0:T(1,128)S(1)} %broadcast_select_fusion.1), channel_id=1, source_target_pairs={{0,4},{1,5},{2,6},{3,7},{4,0},{5,1},{6,2},{7,3},{8,12},{9,13},{10,... | collective-permute-start | bytes 27656 | tf_op jit(solution)/shard_map/cond/branch_1_fun/ppermute | solution.py:157
  36.0 2.8 %token_grad.3 = bf16[256,4608]{1,0:T(8,128)(2,1)} custom-call(bf16[256,4608]{1,0:T(8,128)(2,1)} %get-tuple-element.29.hidden_hbm_ref, f32[1,4608]{1,0:T(1,128)S(1)} %get-tuple-element.30.v_ref, f32[256,128]{1,0:T(8,128)S(1)} %get-tuple-element.31.alpha_ref, f32[256,128]{1,0:T(8,128)S(1)} %get-tuple-element.32.beta_ref), custom_call_target="tpu_custom_call" | custom-call | flops 7077888 | bytes 4718592 | tf_op jit(solution)/shard_map/cond/branch_1_fun/token_grad/pallas_call | solution.py:143
  38.8 0.0 collective-permute-done
  38.8 1.0 %collective-permute-start.1 = (f32[1,1152]{1,0:T(1,128)S(1)}, f32[1,1152]{1,0:T(1,128)S(1)}, u32[]{:S(2)}, u32[]{:S(2)}) collective-permute-start(f32[1,1152]{1,0:T(1,128)S(1)} %broadcast_select_fusion.2), channel_id=1, source_target_pairs={{0,2},{1,3},{2,0},{3,1},{4,6},{5,7},{6,4},{7,5},{8,10},{9,11},{10,... | collective-permute-start | bytes 13832 | tf_op jit(solution)/shard_map/cond/branch_1_fun/ppermute | solution.py:157
  39.8 1.9 %collective-permute-done.1 = f32[1,1152]{1,0:T(1,128)S(1)} collective-permute-done((f32[1,1152]{1,0:T(1,128)S(1)}, f32[1,1152]{1,0:T(1,128)S(1)}, u32[]{:S(2)}, u32[]{:S(2)}) %collective-permute-start.1) | collective-permute-done | bytes 4640 | tf_op jit(solution)/shard_map/cond/branch_1_fun/ppermute | solution.py:157
  41.7 0.1 broadcast_select_fusion.4
  41.8 3.8 %collective-permute-start.2 = (f32[1,576]{1,0:T(1,128)S(1)}, f32[1,576]{1,0:T(1,128)S(1)}, u32[]{:S(2)}, u32[]{:S(2)}) collective-permute-start(f32[1,576]{1,0:T(1,128)S(1)} %broadcast_select_fusion.4), channel_id=1, source_target_pairs={{0,1},{1,0},{2,3},{3,2},{4,5},{5,4},{6,7},{7,6},{8,9},{9,8},{10,11... | collective-permute-start | bytes 6920 | tf_op jit(solution)/shard_map/cond/branch_1_fun/ppermute | solution.py:157
  45.6 0.8 %collective-permute-done.2 = f32[1,576]{1,0:T(1,128)S(1)} collective-permute-done((f32[1,576]{1,0:T(1,128)S(1)}, f32[1,576]{1,0:T(1,128)S(1)}, u32[]{:S(2)}, u32[]{:S(2)}) %collective-permute-start.2) | collective-permute-done | bytes 2336 | tf_op jit(solution)/shard_map/cond/branch_1_fun/ppermute | solution.py:157
  46.4 0.1 fusion.2
  46.5 0.0 all-to-all-done.1.coded_ref
  46.5 0.0 copy-done
  46.5 0.0 copy-done.1
  46.5 0.0 copy-start.2
  46.5 1.3 %copy-done.2 = f32[64,4608]{1,0:T(8,128)S(1)} copy-done((f32[64,4608]{1,0:T(8,128)S(1)}, f32[64,4608]{1,0:T(8,128)}, u32[]{:S(2)}) %copy-start.2) | copy-done | bytes 1179672
  47.8 2.4 %update.1 = (f32[1,576]{1,0:T(1,128)}, f32[1,576]{1,0:T(1,128)}, f32[64,4608]{1,0:T(8,128)}, f32[64,4608]{1,0:T(8,128)}, bf16[64,4608]{1,0:T(8,128)(2,1)}) custom-call(s16[16,8,2432]{2,1,0:T(8,128)(2,1)S(1)} %all-to-all-done.1.coded_ref, f32[1,576]{1,0:T(1,128)S(1)} %get-tuple-element.77.w_ref, f32[1,576]{1,0:T(1,128)S(1)} %broadcast_in_dim.13.gain_ref, ...), custom_call_target="tpu_custom_call" | custom-call | flops 2949120 | bytes 6488064 | tf_op jit(solution)/shard_map/update/pallas_call | solution.py:254
  (15 shorter events, 0.2 us)
Async XLA Ops:
  0.6 7.8 %copy-start.8 = (bf16[576]{0:T(1024)(128)(2,1)S(1)}, bf16[576]{0:T(1024)(128)(2,1)}, u32[]{:S(2)}) copy-start(bf16[576]{0:T(1024)(128)(2,1)} %param.14) | copy-start | bytes 3460
  0.6 7.8 %copy-start.7 = (bf16[576]{0:T(1024)(128)(2,1)S(1)}, bf16[576]{0:T(1024)(128)(2,1)}, u32[]{:S(2)}) copy-start(bf16[576]{0:T(1024)(128)(2,1)} %param.13) | copy-start | bytes 3460
  0.7 25.9 %copy-start.6 = (bf16[256,4608]{1,0:T(8,128)(2,1)S(1)}, bf16[256,4608]{1,0:T(8,128)(2,1)}, u32[]{:S(2)}) copy-start(bf16[256,4608]{1,0:T(8,128)(2,1)} %hidden_ref.1) | copy-start | bytes 7077892
  0.7 18.8 %all-to-all-start = ((bf16[16,8,2304]{2,1,0:T(8,128)(2,1)}), bf16[16,8,2304]{2,1,0:T(8,128)(2,1)S(1)}, u32[]{:S(2)}, u32[]{:S(2)}) async-start(bf16[16,8,2304]{2,1,0:T(8,128)(2,1)} %bitcast.11), calls=%async_computation | async-start | bytes 1179648 | tf_op jit(solution)/shard_map/all_to_all | solution.py:277
  8.4 18.2 %copy-start.4 = (s32[1,8]{1,0:T(1,128)S(1)}, s32[1,8]{1,0:T(1,128)}, u32[]{:S(2)}) copy-start(s32[1,8]{1,0:T(1,128)} %lengths_ref.1) | copy-start | bytes 100
  8.4 18.2 %copy-start.5 = (s32[1,8]{1,0:T(1,128)S(1)}, s32[1,8]{1,0:T(1,128)}, u32[]{:S(2)}) copy-start(s32[1,8]{1,0:T(1,128)} %ranks_ref.1) | copy-start | bytes 100
  8.5 3.8 %collective-permute-start.3 = (f32[1,576]{1,0:T(1,128)S(1)}, f32[1,576]{1,0:T(1,128)S(1)}, u32[]{:S(2)}, u32[]{:S(2)}) collective-permute-start(f32[1,576]{1,0:T(1,128)S(1)} %mul.7), channel_id=1, source_target_pairs={{0,1},{1,0},{2,3},{3,2},{4,5},{5,4},{6,7},{7,6},{8,9},{9,8},{10,11... | collective-permute-start | bytes 6920 | tf_op jit(solution)/shard_map/ppermute | solution.py:157
  12.4 3.0 %collective-permute-start.4 = (f32[1,1152]{1,0:T(1,128)S(1)}, f32[1,1152]{1,0:T(1,128)S(1)}, u32[]{:S(2)}, u32[]{:S(2)}) collective-permute-start(f32[1,1152]{1,0:T(1,128)S(1)} %broadcast_select_fusion.8), channel_id=1, source_target_pairs={{0,2},{1,3},{2,0},{3,1},{4,6},{5,7},{6,4},{7,5},{8,10},{9,11},{10,... | collective-permute-start | bytes 13832 | tf_op jit(solution)/shard_map/ppermute | solution.py:157
  15.4 11.1 %collective-permute-start.5 = (f32[1,2304]{1,0:T(1,128)S(1)}, f32[1,2304]{1,0:T(1,128)S(1)}, u32[]{:S(2)}, u32[]{:S(2)}) collective-permute-start(f32[1,2304]{1,0:T(1,128)S(1)} %broadcast_select_fusion.7), channel_id=1, source_target_pairs={{0,4},{1,5},{2,6},{3,7},{4,0},{5,1},{6,2},{7,3},{8,12},{9,13},{10,... | collective-permute-start | bytes 27656 | tf_op jit(solution)/shard_map/ppermute | solution.py:157
  19.6 10.1 %collective-permute-start.6 = (f32[8,2304]{1,0:T(8,128)S(1)}, f32[8,2304]{1,0:T(8,128)S(1)}, u32[]{:S(2)}, u32[]{:S(2)}) collective-permute-start(f32[8,2304]{1,0:T(8,128)S(1)} %convert_reduce_fusion.near_ref), channel_id=1, source_target_pairs={{0,128},{8,136},{16,144},{24,152},{32,160},{40,168},{48,176},{56,1... | collective-permute-start | bytes 221192 | tf_op jit(solution)/shard_map/ppermute | solution.py:289
  26.6 3.0 %copy-start.3 = (f32[8,2304]{1,0:T(8,128)S(1)}, f32[8,2304]{1,0:T(8,128)}, u32[]{:S(2)}) copy-start(f32[8,2304]{1,0:T(8,128)} %own.1.global_ref) | copy-start | bytes 221188
  30.7 15.8 %all-to-all-start.1 = ((s16[16,8,2432]{2,1,0:T(8,128)(2,1)}), s16[16,8,2432]{2,1,0:T(8,128)(2,1)S(1)}, u32[]{:S(2)}, u32[]{:S(2)}) async-start(s16[16,8,2432]{2,1,0:T(8,128)(2,1)} %average.1), calls=%async_computation.1 | async-start | bytes 1245184 | tf_op jit(solution)/shard_map/all_to_all | solution.py:296
  34.7 11.8 %copy-start = (f32[64,4608]{1,0:T(8,128)S(1)}, f32[64,4608]{1,0:T(8,128)}, u32[]{:S(2)}) copy-start(f32[64,4608]{1,0:T(8,128)} %global_ref.3) | copy-start | bytes 3538948
  34.7 11.8 %copy-start.1 = (bf16[1,64,4608]{2,1,0:T(8,128)(2,1)S(1)}, bf16[1,64,4608]{2,1,0:T(8,128)(2,1)}, u32[]{:S(2)}) copy-start(bf16[1,64,4608]{2,1,0:T(8,128)(2,1)} %param.15) | copy-start | bytes 1769476
  34.8 4.0 %collective-permute-start = (f32[1,2304]{1,0:T(1,128)S(1)}, f32[1,2304]{1,0:T(1,128)S(1)}, u32[]{:S(2)}, u32[]{:S(2)}) collective-permute-start(f32[1,2304]{1,0:T(1,128)S(1)} %broadcast_select_fusion.1), channel_id=1, source_target_pairs={{0,4},{1,5},{2,6},{3,7},{4,0},{5,1},{6,2},{7,3},{8,12},{9,13},{10,... | collective-permute-start | bytes 27656 | tf_op jit(solution)/shard_map/cond/branch_1_fun/ppermute | solution.py:157
  38.8 2.8 %collective-permute-start.1 = (f32[1,1152]{1,0:T(1,128)S(1)}, f32[1,1152]{1,0:T(1,128)S(1)}, u32[]{:S(2)}, u32[]{:S(2)}) collective-permute-start(f32[1,1152]{1,0:T(1,128)S(1)} %broadcast_select_fusion.2), channel_id=1, source_target_pairs={{0,2},{1,3},{2,0},{3,1},{4,6},{5,7},{6,4},{7,5},{8,10},{9,11},{10,... | collective-permute-start | bytes 13832 | tf_op jit(solution)/shard_map/cond/branch_1_fun/ppermute | solution.py:157
  41.8 4.6 %collective-permute-start.2 = (f32[1,576]{1,0:T(1,128)S(1)}, f32[1,576]{1,0:T(1,128)S(1)}, u32[]{:S(2)}, u32[]{:S(2)}) collective-permute-start(f32[1,576]{1,0:T(1,128)S(1)} %broadcast_select_fusion.4), channel_id=1, source_target_pairs={{0,1},{1,0},{2,3},{3,2},{4,5},{5,4},{6,7},{7,6},{8,9},{9,8},{10,11... | collective-permute-start | bytes 6920 | tf_op jit(solution)/shard_map/cond/branch_1_fun/ppermute | solution.py:157
  46.5 1.3 %copy-start.2 = (f32[64,4608]{1,0:T(8,128)S(1)}, f32[64,4608]{1,0:T(8,128)}, u32[]{:S(2)}) copy-start(f32[64,4608]{1,0:T(8,128)} %momentum_ref.1) | copy-start | bytes 3538948

commit v5 on v4

--- a/solution.py
+++ b/solution.py
@@ -209,15 +209,25 @@
     )(near, far, own_global)
 
 
-def update_kernel(coded_ref, w_ref, gain_ref, head_ref, global_ref, momentum_ref, local_ref,
+def update_kernel(coded_ref, w_ref, gain_ref, head_ref, global_ref, scaled_hbm_ref, local_ref,
                   grad_gain_ref, grad_head_ref, *refs):
-    outs, kept, sem = refs[:3], refs[3:6], refs[6]
+    outs, kept, sem, grads, grad_sem, scaled_ref, in_sem = refs[:3], refs[3:6], *refs[6:11]
     rows, width = global_ref.shape
     across = width // BROAD
     new_global_ref, new_momentum_ref, merged_ref = kept
-    copies = []
     band_rows, band_pieces = rows // BANDS, PLANE // BANDS
+    arrivals = []
     for band in range(BANDS):
+        part = pl.ds(band * band_rows, band_rows)
+        arrivals.append(pltpu.make_async_copy(scaled_hbm_ref.at[part], scaled_ref.at[part], in_sem.at[band]))
+        arrivals[-1].start()
+    grads[0] = w_ref[...] * head_ref[...]
+    grads[1] = w_ref[...] * gain_ref[...]
+    copies = [pltpu.make_async_copy(grads.at[n], out, grad_sem.at[n]) for n, out in enumerate((grad_gain_ref, grad_head_ref))]
+    for copy in copies:
+        copy.start()
+    for band in range(BANDS):
+        arrivals[band].wait()
         for p in range(band * band_pieces, (band + 1) * band_pieces):
             row = slice(p // across * TALL, (p // across + 1) * TALL)
             scale = coded_ref[p, :, BROAD:].astype(jnp.int32).astype(jnp.float32) * (LARGEST / (STEPS * STEPS))
@@ -226,7 +236,7 @@
                 part = slice(at, at + LANES)
                 steps = coded_ref[p, :, j * LANES:(j + 1) * LANES].astype(jnp.int32).astype(jnp.float32)
                 average = steps * scale
-                new_momentum = MOMENTUM * momentum_ref[row, part] + average
+                new_momentum = scaled_ref[row, part] + average
                 new_global = global_ref[row, part] - OUTER_RATE * (MOMENTUM * new_momentum + average)
                 new_momentum_ref[row, part] = new_momentum
                 new_global_ref[row, part] = new_global
@@ -238,14 +248,11 @@
         for n in range(3):
             copies.append(pltpu.make_async_copy(kept[n].at[row, :], outs[n].at[row, :], sem.at[n, band]))
             copies[-1].start()
-    w = w_ref[...]
-    grad_gain_ref[...] = w * head_ref[...]
-    grad_head_ref[...] = w * gain_ref[...]
     for copy in copies:
         copy.wait()
 
 
-def update_call(coded, w, gain, head, global_prev, momentum, local):
+def update_call(coded, w, gain, head, global_prev, scaled, local):
     rows, width = global_prev.shape
     vmem = pl.BlockSpec(memory_space=pltpu.VMEM)
     whole = pl.BlockSpec(memory_space=pl.ANY)
@@ -254,14 +261,15 @@
     return pl.pallas_call(
         update_kernel,
         out_shape=(grad, grad) + tuple(jax.ShapeDtypeStruct((rows, width), t) for t in (wide, wide, narrow)),
-        in_specs=[vmem] * 7,
-        out_specs=(vmem,) * 2 + (whole,) * 3,
+        in_specs=[vmem] * 5 + [whole, vmem],
+        out_specs=(whole,) * 5,
         scratch_shapes=[pltpu.VMEM((rows, width), t) for t in (wide, wide, narrow)]
-        + [pltpu.SemaphoreType.DMA((3, BANDS))],
+        + [pltpu.SemaphoreType.DMA((3, BANDS)), pltpu.VMEM((2, *w.shape), wide), pltpu.SemaphoreType.DMA((2,))]
+        + [pltpu.VMEM((rows, width), wide), pltpu.SemaphoreType.DMA((BANDS,))],
         compiler_params=pltpu.CompilerParams(vmem_limit_bytes=VMEM_LIMIT),
         cost_estimate=pl.CostEstimate(flops=10 * rows * width, bytes_accessed=22 * rows * width, transcendentals=0),
         name="update",
-    )(coded, w, gain, head, global_prev, momentum, local)
+    )(coded, w, gain, head, global_prev, scaled, local)
 
 
 def body(hidden, lengths, ranks, gain, head, local_frag, global_prev, momentum):
@@ -295,28 +303,31 @@
     coded, w = barrier((coded, w))
     received = lax.all_to_all(coded, "rep", 0, 0, tiled=True, axis_index_groups=planes)
 
-    def halve(hidden, v, alpha, beta, w):
-        d_hidden = None
+    def halve(hidden, v, alpha, beta, momentum, w):
+        d_hidden = token_call(hidden, v, alpha, beta)
+        scaled = MOMENTUM * momentum
         for bit in (4, 2, 1):
             half = w.shape[1] // 2
             low, high = w[:, :half], w[:, half:]
             kept, sent = jnp.where(here & bit == 0, low, high), jnp.where(here & bit == 0, high, low)
             term = along(sent, bit)
             if bit == 4:
-                d_hidden = token_call(hidden, v, alpha, beta)
-                term, d_hidden = barrier((term, d_hidden))
+                term, d_hidden, momentum = barrier((term, d_hidden, momentum))
+                scaled = MOMENTUM * momentum
+            if bit == 2:
+                term, scaled = barrier((term, scaled))
             w = kept + term
-        return d_hidden, w
-
-    def no_halving(hidden, v, alpha, beta, w):
-        return token_call(hidden, v, alpha, beta), w[:, :w.shape[1] // devices]
-
-    d_hidden, w = lax.cond(
-        lax.axis_index("rep") < replicas, halve, no_halving, hidden, v, alpha, beta, w
+        return d_hidden, scaled, w
+
+    def no_halving(hidden, v, alpha, beta, momentum, w):
+        return token_call(hidden, v, alpha, beta), MOMENTUM * momentum, w[:, :w.shape[1] // devices]
+
+    d_hidden, scaled, w = lax.cond(
+        lax.axis_index("rep") < replicas, halve, no_halving, hidden, v, alpha, beta, momentum, w
     )
 
     grad_gain, grad_head, new_global, new_momentum, merged = update_call(
-        received, w, gain_wide, head_wide, global_prev, momentum, local
+        received, w, gain_wide, head_wide, global_prev, scaled, local
     )
     return d_hidden, grad_gain, grad_head, new_global, new_momentum, merged[None]
 

time: 50.6 us -> 49.8 us (0.984)
  local copies, waits for them, and re-layouts: 1.34 us -> 0.08 us
  other arithmetic: 1.1 us -> 2.24 us
  waiting for transfers between devices: 4.87 us -> 3.79 us
    unnamed x18 -> x16, local copies, waits for them, and re-layouts: 1.31 us -> 0.05 us
    mul x0 -> x1, other arithmetic: none -> 1.15 us  [halve(): scaled = MOMENTUM * momentum]
    ppermute x6, waiting for transfers between devices: 3.91 us -> 2.83 us  [along(): return lax.ppermute(array, 'fsdp', [(i, i ^ k) for i in range(devices)])]
  transfers between devices with their start and end apart: 9 -> 9, of which waited for: 4 -> 4; matrix products, arithmetic and copies ran while one was open for 2% -> 5% of each run, Pallas kernels for 16% -> 16%
where the time goes in v5:
time: 49.8 us; the launch traced here: 49.4 us
  starting transfers between devices  30.5 us (61%)
  Pallas kernels  11.8 us (24%)
  waiting for transfers between devices  3.79 us (8%)
  other arithmetic  2.24 us (4%)
  between operations  0.88 us (2%)
    ppermute x6, starting transfers between devices, along(): return lax.ppermute(array, 'fsdp', [(i, i ^ k) for i in range(devices)])  11.8 us
    all_to_all x1, starting transfers between devices, body(): lax.all_to_all(pieces, 'rep', 0, 0, tiled=True, axis_index_groups=planes)  7.73 us
    ppermute x1, starting transfers between devices, body(): lax.ppermute(near, 'rep', [(i, (i + PLANE) % replicas) for i in range(rep...  7 us
    all_to_all x1, starting transfers between devices, body(): lax.all_to_all(coded, 'rep', 0, 0, tiled=True, axis_index_groups=planes)  4.02 us
    pallas_call x1, Pallas kernels, score_call(): pl.pallas_call(score_kernel, out_shape=(wide, wide, jax.ShapeDtypeStruct(...  2.99 us
    pallas_call x1, Pallas kernels, token_call(): pl.pallas_call(token_kernel, out_shape=jax.ShapeDtypeStruct((tokens, widt...  2.85 us
    ppermute x6, waiting for transfers between devices, along(): return lax.ppermute(array, 'fsdp', [(i, i ^ k) for i in range(devices)])  2.83 us
    pallas_call x1, Pallas kernels, update_call(): pl.pallas_call(update_kernel, out_shape=(grad, grad) + tuple((jax.ShapeDt...  2.8 us
  transfers between devices with their start and end apart: 9, of which 4 were waited for; matrix products, arithmetic and copies ran while one was open for 5% of the time, Pallas kernels for 16%

profile of v5, /device:TPU:1, one launch (start us, length us, event | category | flops | bytes accessed | tf_op | source)
XLA Modules:
  0.0 49.4 jit_solution(9811554398612032936)
XLA Ops:
  0.6 0.0 copy-start.8
  0.6 0.0 copy-start.9
  0.7 0.0 copy-start.5
  0.7 7.7 %all-to-all-start = ((bf16[16,8,2304]{2,1,0:T(8,128)(2,1)}), bf16[16,8,2304]{2,1,0:T(8,128)(2,1)S(1)}, u32[]{:S(2)}, u32[]{:S(2)}) async-start(bf16[16,8,2304]{2,1,0:T(8,128)(2,1)} %bitcast.11), calls=%async_computation | async-start | bytes 1179648 | tf_op jit(solution)/shard_map/all_to_all | solution.py:285
  8.4 0.0 copy-done.8
  8.4 0.0 copy-done.9
  8.4 0.0 copy-start.3
  8.4 0.0 copy-start.4
  8.5 1.0 %collective-permute-start.3 = (f32[1,576]{1,0:T(1,128)S(1)}, f32[1,576]{1,0:T(1,128)S(1)}, u32[]{:S(2)}, u32[]{:S(2)}) collective-permute-start(f32[1,576]{1,0:T(1,128)S(1)} %mul.13), channel_id=1, source_target_pairs={{0,1},{1,0},{2,3},{3,2},{4,5},{5,4},{6,7},{7,6},{8,9},{9,8},{10,11... | collective-permute-start | bytes 6920 | tf_op jit(solution)/shard_map/ppermute | solution.py:157
  9.5 0.6 %add_bitcast_fusion.at_ref = s32[1,2]{1,0:T(1,128)} fusion(s32[1]{0:T(128)} %bitcast.4, s32[1]{0:T(128)} %bitcast.3), kind=kLoop, calls=%fused_computation.18 | loop fusion | flops 2 | bytes 16 | tf_op jit(solution)/shard_map/broadcast_in_dim | solution.py:293
  10.1 2.2 %own.1.global_ref = f32[8,2304]{1,0:T(8,128)} custom-call(s32[1,2]{1,0:T(1,128)} %add_bitcast_fusion.at_ref, f32[64,4608]{1,0:T(8,128)} %global_ref.3), custom_call_target="tpu_custom_call" | custom-call | bytes 147456 | tf_op jit(solution)/shard_map/own/pallas_call | solution.py:169
  12.3 0.0 collective-permute-done.3
  12.3 0.1 broadcast_select_fusion.8
  12.4 1.7 %collective-permute-start.4 = (f32[1,1152]{1,0:T(1,128)S(1)}, f32[1,1152]{1,0:T(1,128)S(1)}, u32[]{:S(2)}, u32[]{:S(2)}) collective-permute-start(f32[1,1152]{1,0:T(1,128)S(1)} %broadcast_select_fusion.8), channel_id=1, source_target_pairs={{0,2},{1,3},{2,0},{3,1},{4,6},{5,7},{6,4},{7,5},{8,10},{9,11},{10,... | collective-permute-start | bytes 13832 | tf_op jit(solution)/shard_map/ppermute | solution.py:157
  14.1 0.1 maximum_select_fusion.1
  14.2 1.2 %collective-permute-done.4 = f32[1,1152]{1,0:T(1,128)S(1)} collective-permute-done((f32[1,1152]{1,0:T(1,128)S(1)}, f32[1,1152]{1,0:T(1,128)S(1)}, u32[]{:S(2)}, u32[]{:S(2)}) %collective-permute-start.4) | collective-permute-done | bytes 4640 | tf_op jit(solution)/shard_map/ppermute | solution.py:157
  15.4 3.1 %collective-permute-start.5 = (f32[1,2304]{1,0:T(1,128)S(1)}, f32[1,2304]{1,0:T(1,128)S(1)}, u32[]{:S(2)}, u32[]{:S(2)}) collective-permute-start(f32[1,2304]{1,0:T(1,128)S(1)} %broadcast_select_fusion.7), channel_id=1, source_target_pairs={{0,4},{1,5},{2,6},{3,7},{4,0},{5,1},{6,2},{7,3},{8,12},{9,13},{10,... | collective-permute-start | bytes 27656 | tf_op jit(solution)/shard_map/ppermute | solution.py:157
  18.5 1.0 %all-to-all-done = bf16[16,8,2304]{2,1,0:T(8,128)(2,1)S(1)} async-done(((bf16[16,8,2304]{2,1,0:T(8,128)(2,1)}), bf16[16,8,2304]{2,1,0:T(8,128)(2,1)S(1)}, u32[]{:S(2)}, u32[]{:S(2)}) %all-to-all-start) | async-done | bytes 589856 | tf_op jit(solution)/shard_map/all_to_all | solution.py:285
  19.5 0.1 convert_reduce_fusion.near_ref
  19.6 7.0 %collective-permute-start.6 = (f32[8,2304]{1,0:T(8,128)S(1)}, f32[8,2304]{1,0:T(8,128)S(1)}, u32[]{:S(2)}, u32[]{:S(2)}) collective-permute-start(f32[8,2304]{1,0:T(8,128)S(1)} %convert_reduce_fusion.near_ref), channel_id=1, source_target_pairs={{0,128},{8,136},{16,144},{24,152},{32,160},{40,168},{48,176},{56,1... | collective-permute-start | bytes 221192 | tf_op jit(solution)/shard_map/ppermute | solution.py:297
  26.5 0.0 collective-permute-done.5
  26.6 0.0 copy-done.5
  26.6 0.0 copy-done.3
  26.6 0.0 copy-done.4
  26.6 0.0 copy-start.2
  26.6 3.0 %score.1 = (f32[256,128]{1,0:T(8,128)S(1)}, f32[256,128]{1,0:T(8,128)S(1)}, f32[1,4608]{1,0:T(1,128)S(1)}) custom-call(s32[1,8]{1,0:T(1,128)S(1)} %copy-done.3, s32[1,8]{1,0:T(1,128)S(1)} %copy-done.4, bf16[256,4608]{1,0:T(8,128)(2,1)S(1)} %copy-done.5, f32[1,4608]{1,0:T(1,128)S(1)} %broadcast_select_fusion.6.v_ref), custom_call_target="tpu_custom_call" | custom-call | flops 7077888 | bytes 2359296 | tf_op jit(solution)/shard_map/score/pallas_call | solution.py:104
  29.6 0.0 collective-permute-done.6.far_ref
  29.6 0.0 copy-done.2
  29.6 1.0 %average.1 = s16[16,8,2432]{2,1,0:T(8,128)(2,1)} custom-call(f32[8,2304]{1,0:T(8,128)S(1)} %convert_reduce_fusion.near_ref, f32[8,2304]{1,0:T(8,128)S(1)} %collective-permute-done.6.far_ref, f32[8,2304]{1,0:T(8,128)S(1)} %copy-done.2), custom_call_target="tpu_custom_call" | custom-call | flops 184320 | bytes 737280 | tf_op jit(solution)/shard_map/average/pallas_call | solution.py:200
  30.6 4.0 %all-to-all-start.1 = ((s16[16,8,2432]{2,1,0:T(8,128)(2,1)}), s16[16,8,2432]{2,1,0:T(8,128)(2,1)S(1)}, u32[]{:S(2)}, u32[]{:S(2)}) async-start(s16[16,8,2432]{2,1,0:T(8,128)(2,1)} %average.1), calls=%async_computation.1 | async-start | bytes 1245184 | tf_op jit(solution)/shard_map/all_to_all | solution.py:304
  34.7 0.0 copy-start
  34.7 0.0 copy-start.1
  34.7 11.9 %conditional.1 = (bf16[256,4608]{1,0:T(8,128)(2,1)}, f32[64,4608]{1,0:T(8,128)}, f32[1,576]{1,0:T(1,128)S(1)}) conditional(s32[]{:T(128)} %convert_element_type.12, (bf16[256,4608]{1,0:T(8,128)(2,1)}, f32[1,4608]{1,0:T(1,128)S(1)}, f32[256,128]{1,0:T(8,128)S(1)}, f32[256,128]{1,0:T(8,128)S(1)}, f32[64,4608]{1,0:T(8,128)}, ...), branch_computations={%region_1.2_spmd, %region_2.3_spmd} | conditional | flops 7384902 | bytes 11974129 | solution.py:325
  34.7 1.3 %collective-permute-start = (f32[1,2304]{1,0:T(1,128)S(1)}, f32[1,2304]{1,0:T(1,128)S(1)}, u32[]{:S(2)}, u32[]{:S(2)}) collective-permute-start(f32[1,2304]{1,0:T(1,128)S(1)} %broadcast_select_fusion.1), channel_id=1, source_target_pairs={{0,4},{1,5},{2,6},{3,7},{4,0},{5,1},{6,2},{7,3},{8,12},{9,13},{10,... | collective-permute-start | bytes 27656 | tf_op jit(solution)/shard_map/cond/branch_1_fun/ppermute | solution.py:157
  36.0 2.8 %token_grad.3 = bf16[256,4608]{1,0:T(8,128)(2,1)} custom-call(bf16[256,4608]{1,0:T(8,128)(2,1)} %get-tuple-element.34.hidden_hbm_ref, f32[1,4608]{1,0:T(1,128)S(1)} %get-tuple-element.35.v_ref, f32[256,128]{1,0:T(8,128)S(1)} %get-tuple-element.36.alpha_ref, f32[256,128]{1,0:T(8,128)S(1)} %get-tuple-element.37.beta_ref), custom_call_target="tpu_custom_call" | custom-call | flops 7077888 | bytes 4718592 | tf_op jit(solution)/shard_map/cond/branch_1_fun/token_grad/pallas_call | solution.py:143
  38.9 0.0 collective-permute-done
  38.9 0.9 %collective-permute-start.1 = (f32[1,1152]{1,0:T(1,128)S(1)}, f32[1,1152]{1,0:T(1,128)S(1)}, u32[]{:S(2)}, u32[]{:S(2)}) collective-permute-start(f32[1,1152]{1,0:T(1,128)S(1)} %broadcast_select_fusion.3), channel_id=1, source_target_pairs={{0,2},{1,3},{2,0},{3,1},{4,6},{5,7},{6,4},{7,5},{8,10},{9,11},{10,... | collective-permute-start | bytes 13832 | tf_op jit(solution)/shard_map/cond/branch_1_fun/ppermute | solution.py:157
  39.8 0.0 copy-done.7
  39.8 1.1 %broadcast_multiply_fusion.1 = f32[64,4608]{1,0:T(8,128)} fusion(f32[64,4608]{1,0:T(8,128)S(1)} %copy-done.7), kind=kLoop, calls=%fused_computation.1 | loop fusion | flops 294912 | bytes 2359296 | tf_op jit(solution)/shard_map/cond/branch_1_fun/mul | solution.py:316
  40.9 0.8 %collective-permute-done.1 = f32[1,1152]{1,0:T(1,128)S(1)} collective-permute-done((f32[1,1152]{1,0:T(1,128)S(1)}, f32[1,1152]{1,0:T(1,128)S(1)}, u32[]{:S(2)}, u32[]{:S(2)}) %collective-permute-start.1) | collective-permute-done | bytes 4640 | tf_op jit(solution)/shard_map/cond/branch_1_fun/ppermute | solution.py:157
  41.8 0.1 broadcast_select_fusion.4
  41.8 3.8 %collective-permute-start.2 = (f32[1,576]{1,0:T(1,128)S(1)}, f32[1,576]{1,0:T(1,128)S(1)}, u32[]{:S(2)}, u32[]{:S(2)}) collective-permute-start(f32[1,576]{1,0:T(1,128)S(1)} %broadcast_select_fusion.4), channel_id=1, source_target_pairs={{0,1},{1,0},{2,3},{3,2},{4,5},{5,4},{6,7},{7,6},{8,9},{9,8},{10,11... | collective-permute-start | bytes 6920 | tf_op jit(solution)/shard_map/cond/branch_1_fun/ppermute | solution.py:157
  45.7 0.8 %collective-permute-done.2 = f32[1,576]{1,0:T(1,128)S(1)} collective-permute-done((f32[1,576]{1,0:T(1,128)S(1)}, f32[1,576]{1,0:T(1,128)S(1)}, u32[]{:S(2)}, u32[]{:S(2)}) %collective-permute-start.2) | collective-permute-done | bytes 2336 | tf_op jit(solution)/shard_map/cond/branch_1_fun/ppermute | solution.py:157
  46.5 0.1 fusion.2
  46.6 0.0 all-to-all-done.1.coded_ref
  46.6 0.0 copy-done
  46.6 0.0 copy-done.1
  46.6 2.8 %update.1 = (f32[1,576]{1,0:T(1,128)}, f32[1,576]{1,0:T(1,128)}, f32[64,4608]{1,0:T(8,128)}, f32[64,4608]{1,0:T(8,128)}, bf16[64,4608]{1,0:T(8,128)(2,1)}) custom-call(s16[16,8,2432]{2,1,0:T(8,128)(2,1)S(1)} %all-to-all-done.1.coded_ref, f32[1,576]{1,0:T(1,128)S(1)} %get-tuple-element.87.w_ref, f32[1,576]{1,0:T(1,128)S(1)} %broadcast_in_dim.13.gain_ref, ...), custom_call_target="tpu_custom_call" | custom-call | flops 2949120 | bytes 6488064 | tf_op jit(solution)/shard_map/update/pallas_call | solution.py:261
  (16 shorter events, 0.2 us)
Async XLA Ops:
  0.6 7.8 %copy-start.8 = (bf16[576]{0:T(1024)(128)(2,1)S(1)}, bf16[576]{0:T(1024)(128)(2,1)}, u32[]{:S(2)}) copy-start(bf16[576]{0:T(1024)(128)(2,1)} %param.13) | copy-start | bytes 3460
  0.6 7.8 %copy-start.9 = (bf16[576]{0:T(1024)(128)(2,1)S(1)}, bf16[576]{0:T(1024)(128)(2,1)}, u32[]{:S(2)}) copy-start(bf16[576]{0:T(1024)(128)(2,1)} %param.14) | copy-start | bytes 3460
  0.7 25.9 %copy-start.5 = (bf16[256,4608]{1,0:T(8,128)(2,1)S(1)}, bf16[256,4608]{1,0:T(8,128)(2,1)}, u32[]{:S(2)}) copy-start(bf16[256,4608]{1,0:T(8,128)(2,1)} %hidden_ref.1) | copy-start | bytes 7077892
  0.7 18.8 %all-to-all-start = ((bf16[16,8,2304]{2,1,0:T(8,128)(2,1)}), bf16[16,8,2304]{2,1,0:T(8,128)(2,1)S(1)}, u32[]{:S(2)}, u32[]{:S(2)}) async-start(bf16[16,8,2304]{2,1,0:T(8,128)(2,1)} %bitcast.11), calls=%async_computation | async-start | bytes 1179648 | tf_op jit(solution)/shard_map/all_to_all | solution.py:285
  8.4 18.2 %copy-start.3 = (s32[1,8]{1,0:T(1,128)S(1)}, s32[1,8]{1,0:T(1,128)}, u32[]{:S(2)}) copy-start(s32[1,8]{1,0:T(1,128)} %lengths_ref.1) | copy-start | bytes 100
  8.4 18.2 %copy-start.4 = (s32[1,8]{1,0:T(1,128)S(1)}, s32[1,8]{1,0:T(1,128)}, u32[]{:S(2)}) copy-start(s32[1,8]{1,0:T(1,128)} %ranks_ref.1) | copy-start | bytes 100
  8.5 3.8 %collective-permute-start.3 = (f32[1,576]{1,0:T(1,128)S(1)}, f32[1,576]{1,0:T(1,128)S(1)}, u32[]{:S(2)}, u32[]{:S(2)}) collective-permute-start(f32[1,576]{1,0:T(1,128)S(1)} %mul.13), channel_id=1, source_target_pairs={{0,1},{1,0},{2,3},{3,2},{4,5},{5,4},{6,7},{7,6},{8,9},{9,8},{10,11... | collective-permute-start | bytes 6920 | tf_op jit(solution)/shard_map/ppermute | solution.py:157
  12.4 3.0 %collective-permute-start.4 = (f32[1,1152]{1,0:T(1,128)S(1)}, f32[1,1152]{1,0:T(1,128)S(1)}, u32[]{:S(2)}, u32[]{:S(2)}) collective-permute-start(f32[1,1152]{1,0:T(1,128)S(1)} %broadcast_select_fusion.8), channel_id=1, source_target_pairs={{0,2},{1,3},{2,0},{3,1},{4,6},{5,7},{6,4},{7,5},{8,10},{9,11},{10,... | collective-permute-start | bytes 13832 | tf_op jit(solution)/shard_map/ppermute | solution.py:157
  15.4 11.1 %collective-permute-start.5 = (f32[1,2304]{1,0:T(1,128)S(1)}, f32[1,2304]{1,0:T(1,128)S(1)}, u32[]{:S(2)}, u32[]{:S(2)}) collective-permute-start(f32[1,2304]{1,0:T(1,128)S(1)} %broadcast_select_fusion.7), channel_id=1, source_target_pairs={{0,4},{1,5},{2,6},{3,7},{4,0},{5,1},{6,2},{7,3},{8,12},{9,13},{10,... | collective-permute-start | bytes 27656 | tf_op jit(solution)/shard_map/ppermute | solution.py:157
  19.6 10.1 %collective-permute-start.6 = (f32[8,2304]{1,0:T(8,128)S(1)}, f32[8,2304]{1,0:T(8,128)S(1)}, u32[]{:S(2)}, u32[]{:S(2)}) collective-permute-start(f32[8,2304]{1,0:T(8,128)S(1)} %convert_reduce_fusion.near_ref), channel_id=1, source_target_pairs={{0,128},{8,136},{16,144},{24,152},{32,160},{40,168},{48,176},{56,1... | collective-permute-start | bytes 221192 | tf_op jit(solution)/shard_map/ppermute | solution.py:297
  26.6 3.0 %copy-start.2 = (f32[8,2304]{1,0:T(8,128)S(1)}, f32[8,2304]{1,0:T(8,128)}, u32[]{:S(2)}) copy-start(f32[8,2304]{1,0:T(8,128)} %own.1.global_ref) | copy-start | bytes 221188
  30.6 16.0 %all-to-all-start.1 = ((s16[16,8,2432]{2,1,0:T(8,128)(2,1)}), s16[16,8,2432]{2,1,0:T(8,128)(2,1)S(1)}, u32[]{:S(2)}, u32[]{:S(2)}) async-start(s16[16,8,2432]{2,1,0:T(8,128)(2,1)} %average.1), calls=%async_computation.1 | async-start | bytes 1245184 | tf_op jit(solution)/shard_map/all_to_all | solution.py:304
  34.7 11.9 %copy-start = (f32[64,4608]{1,0:T(8,128)S(1)}, f32[64,4608]{1,0:T(8,128)}, u32[]{:S(2)}) copy-start(f32[64,4608]{1,0:T(8,128)} %global_ref.3) | copy-start | bytes 3538948
  34.7 11.9 %copy-start.1 = (bf16[1,64,4608]{2,1,0:T(8,128)(2,1)S(1)}, bf16[1,64,4608]{2,1,0:T(8,128)(2,1)}, u32[]{:S(2)}) copy-start(bf16[1,64,4608]{2,1,0:T(8,128)(2,1)} %param.15) | copy-start | bytes 1769476
  34.7 4.1 %collective-permute-start = (f32[1,2304]{1,0:T(1,128)S(1)}, f32[1,2304]{1,0:T(1,128)S(1)}, u32[]{:S(2)}, u32[]{:S(2)}) collective-permute-start(f32[1,2304]{1,0:T(1,128)S(1)} %broadcast_select_fusion.1), channel_id=1, source_target_pairs={{0,4},{1,5},{2,6},{3,7},{4,0},{5,1},{6,2},{7,3},{8,12},{9,13},{10,... | collective-permute-start | bytes 27656 | tf_op jit(solution)/shard_map/cond/branch_1_fun/ppermute | solution.py:157
  36.0 3.8 %copy-start.7 = (f32[64,4608]{1,0:T(8,128)S(1)}, f32[64,4608]{1,0:T(8,128)}, u32[]{:S(2)}) copy-start(f32[64,4608]{1,0:T(8,128)} %get-tuple-element.41) | copy-start | bytes 3538948 | tf_op jit(solution)/shard_map/cond
  38.9 2.8 %collective-permute-start.1 = (f32[1,1152]{1,0:T(1,128)S(1)}, f32[1,1152]{1,0:T(1,128)S(1)}, u32[]{:S(2)}, u32[]{:S(2)}) collective-permute-start(f32[1,1152]{1,0:T(1,128)S(1)} %broadcast_select_fusion.3), channel_id=1, source_target_pairs={{0,2},{1,3},{2,0},{3,1},{4,6},{5,7},{6,4},{7,5},{8,10},{9,11},{10,... | collective-permute-start | bytes 13832 | tf_op jit(solution)/shard_map/cond/branch_1_fun/ppermute | solution.py:157
  41.8 4.7 %collective-permute-start.2 = (f32[1,576]{1,0:T(1,128)S(1)}, f32[1,576]{1,0:T(1,128)S(1)}, u32[]{:S(2)}, u32[]{:S(2)}) collective-permute-start(f32[1,576]{1,0:T(1,128)S(1)} %broadcast_select_fusion.4), channel_id=1, source_target_pairs={{0,1},{1,0},{2,3},{3,2},{4,5},{5,4},{6,7},{7,6},{8,9},{9,8},{10,11... | collective-permute-start | bytes 6920 | tf_op jit(solution)/shard_map/cond/branch_1_fun/ppermute | solution.py:157
